TPU v7x, 512 devices: a whole 4x4x16 slice. The times are simulated.
512 devices in a mesh: row: 32 (over x_hi, z), col: 16 (over y, x_lo, core).
Axes of the slice: x: 4 (x_hi: 2, x_lo: 2; x = x_hi * 2 + x_lo), y: 4, z: 16, core: 2. Of those that a mesh axis runs over, the one named last changes fastest.
Arguments:
- traces: float32 [16, 128, 2, 1536], P('col', 'row'), may hold values from -140 to 140
- alive_mask: int32 [16, 128], P('col', 'row'), may hold values 0 or 1
- keep_mask: int32 [16, 128, 2], P('col', 'row'), may hold values 0 or 1
Outputs:
- stacked: float32 [101, 2048, 2048], P(None, 'row', 'col')
All inputs are finite; a program needn't handle non-finite values. No bound on the sum of `alive_mask` or of `keep_mask` on one device may be relied on, other than what follows from the above.
Results may differ from a plain program's by a relative error of at most 0.0058.
Values may be sent and summed in bfloat16 or wider, within the bound.
No kernel may reach another device: no remote copies, remote signals or barrier semaphores. Data moves between devices by JAX's collectives and lax.ppermute only.
A program may use at most 64 MiB of HBM per device.

v0:
```python
import math

import jax
import jax.numpy as jnp
from jax import lax
from jax.sharding import PartitionSpec as P

NT = 1536
NF = 640
SMOOTH = 65
MAXLAG = 50
LAGS = 101


epsilon = 1e-05


def broadcast(value, axis, source):
    kept = jnp.where(lax.axis_index(axis) == source, value, 0).astype(value.dtype)
    return lax.psum(kept, axis)


def fourier_table(samples, bin_count):
    sample_index = jnp.arange(samples, dtype=jnp.int32)[:, None]
    bin_index = jnp.arange(1, bin_count + 1, dtype=jnp.int32)[None, :]
    phases = (sample_index * bin_index % samples).astype(jnp.float32) * (2.0 * math.pi / samples)
    scaling = 1.0 / math.sqrt(samples)
    return jnp.concatenate([jnp.cos(phases), -jnp.sin(phases)], axis=1) * scaling


def band_table(bin_count, span):
    column = jnp.arange(bin_count, dtype=jnp.int32)
    window_start = jnp.clip(column - span // 2, 0, bin_count - span)
    row_index = jnp.arange(bin_count, dtype=jnp.int32)[:, None]
    inside = (row_index >= window_start[None, :]) & (row_index < window_start[None, :] + span)
    return inside.astype(jnp.float32) / span


def lag_table(bin_count, samples, max_lag):
    lag_index = jnp.arange(-max_lag, max_lag + 1, dtype=jnp.int32)[:, None]
    bin_index = jnp.arange(1, bin_count + 1, dtype=jnp.int32)[None, :]
    phases = (lag_index * bin_index % samples).astype(jnp.float32) * (2.0 * math.pi / samples)
    scaling = 1.0 / math.sqrt(bin_count)
    return (jnp.concatenate([jnp.cos(phases), -jnp.sin(phases)], axis=1) * scaling).astype(
        jnp.bfloat16
    )


def whiten(series, weight, fourier, band_matrix):
    spectra = jnp.einsum("cwt,tk->wkc", series, fourier, precision=lax.Precision.HIGHEST)
    bin_count = band_matrix.shape[0]
    real_part = spectra[:, :bin_count]
    imag_part = spectra[:, bin_count:]
    amplitude = jnp.sqrt(real_part * real_part + imag_part * imag_part)
    smooth = jnp.einsum("wfc,fg->wgc", amplitude, band_matrix, precision=lax.Precision.HIGHEST)
    factor = jnp.transpose(weight)[:, None, :] / (smooth + epsilon)
    return (spectra * jnp.concatenate([factor, factor], axis=1)).astype(jnp.bfloat16)


def correlate_group(first_group, partner, lags):
    bin_count = first_group.shape[0] // 2
    first_real = first_group[:bin_count].astype(jnp.float32)[:, :, None]
    first_imag = first_group[bin_count:].astype(jnp.float32)[:, :, None]
    partner_real = partner[:bin_count].astype(jnp.float32)[:, None, :]
    partner_imag = partner[bin_count:].astype(jnp.float32)[:, None, :]
    cross = jnp.concatenate(
        [
            first_real * partner_real + first_imag * partner_imag,
            first_imag * partner_real - first_real * partner_imag,
        ],
        axis=0,
    ).astype(jnp.bfloat16)
    flat = cross.reshape(2 * bin_count, first_group.shape[1] * partner.shape[1])
    result = jnp.dot(lags, flat, preferred_element_type=jnp.float32)
    return result.reshape(lags.shape[0], first_group.shape[1], partner.shape[1])


def correlate(first_block, partner, lags):
    rows = first_block.shape[1]
    group = math.gcd(rows, 16)
    groups = rows // group
    stacked_groups = jnp.transpose(
        first_block.reshape(first_block.shape[0], groups, group), (1, 0, 2)
    )
    results = lax.map(lambda piece: correlate_group(piece, partner, lags), stacked_groups)
    return jnp.transpose(results, (1, 0, 2, 3)).reshape(lags.shape[0], rows, partner.shape[1])


def local(traces, alive_mask, keep_mask):
    row_count = lax.axis_size("row")
    col_count = lax.axis_size("col")
    row_place = lax.axis_index("row")
    own_series = traces[0]
    own_width = own_series.shape[0]
    window_count = own_series.shape[1]
    block_width = own_width * row_count
    first_width = own_width * col_count
    source_block = row_place * first_width // block_width
    source_offset = row_place * first_width % block_width
    weight = alive_mask[0][:, None] * keep_mask[0]
    fourier = fourier_table(NT, NF)
    band_matrix = band_table(NF, SMOOTH)
    lags = lag_table(NF, NT, MAXLAG)
    summed = jnp.zeros((LAGS, first_width, block_width), jnp.float32)
    counts = jnp.zeros((first_width, block_width), jnp.float32)
    for window in range(window_count):
        partner_series, partner_weight = (
            lax.all_gather(own_series[:, window : window + 1], "row", axis=0, tiled=True),
            lax.all_gather(weight[:, window], "row", axis=0, tiled=True),
        )
        first_series, first_weight = (
            broadcast(
                lax.dynamic_slice_in_dim(partner_series, source_offset, first_width, 0),
                "col",
                source_block,
            ),
            broadcast(
                lax.dynamic_slice_in_dim(partner_weight, source_offset, first_width, 0),
                "col",
                source_block,
            ),
        )
        partner = whiten(
            partner_series, partner_weight[:, None].astype(jnp.float32), fourier, band_matrix
        )[0]
        first_block = whiten(
            first_series, first_weight[:, None].astype(jnp.float32), fourier, band_matrix
        )[0]
        summed = summed + correlate(first_block, partner, lags)
        counts = (
            counts
            + first_weight.astype(jnp.float32)[:, None]
            * partner_weight.astype(jnp.float32)[None, :]
        )
    return summed / jnp.maximum(counts, 1.0)


def solution(mesh):
    placed = (P("col", "row", None, None), P("col", "row"), P("col", "row", None))
    return jax.shard_map(
        local, mesh=mesh, in_specs=placed, out_specs=P(None, "row", "col"), check_vma=False
    )
```

profile of v0, /device:TPU:1, one launch (start us, length us, event | category | flops | bytes accessed | tf_op | source)
XLA Modules:
  0.0 401.1 jit_solution(12120920138779407992)
XLA Ops:
  7.5 73.6 %all_gather.14 = f32[128,1,1536]{2,1,0:T(1,128)S(1)} all-gather(f32[4,1,1536]{2,1,0:T(1,128)S(1)} %get-tuple-element.103), channel_id=1, replica_groups=mesh['row'=32,'col'=16] {'row'}, dimensions={0}, use_global_device_ids=true | all-gather | bytes 811008 | tf_op jit(solution)/shard_map/all_gather | solution.py:108
  82.2 61.5 %all_gather.12 = f32[128,1,1536]{2,1,0:T(1,128)S(1)} all-gather(f32[4,1,1536]{2,1,0:T(1,128)S(1)} %get-tuple-element.104), channel_id=1, replica_groups=mesh['row'=32,'col'=16] {'row'}, dimensions={0}, use_global_device_ids=true | all-gather | bytes 811008 | tf_op jit(solution)/shard_map/all_gather | solution.py:108
  144.9 1.3 dynamic-slice.2
  147.1 16.0 %all-reduce.2 = (s32[128]{0:T(128)S(1)}, s32[128]{0:T(128)S(1)}) all-reduce(s32[128]{0:T(128)S(1)} %bitcast_dynamic-update-slice_fusion.3, s32[128]{0:T(128)S(1)} %bitcast_dynamic-update-slice_fusion.2), channel_id=2, replica_groups=mesh['row'=32,'col'=16] {'row'}, use_global_device_ids=true, to_apply=%add | all-reduce | flops 256 | bytes 2048
  163.3 16.2 %fusion.18 = (f32[1536,640]{1,0:T(8,128)S(1)}, f32[1536,640]{1,0:T(8,128)S(1)}) fusion(s32[640]{0:T(1024)S(1)} %iota_add_fusion), kind=kLoop, calls=%fused_computation.40 | loop fusion | flops 9830400 | bytes 7866880 | tf_op jit(solution)/shard_map/cos | solution.py:28
  179.5 12.8 %fusion.30 = f32[1280,128]{1,0:T(8,128)S(1)} fusion(f32[1536,640]{1,0:T(8,128)S(1)} %get-tuple-element.108, f32[1536,640]{1,0:T(8,128)S(1)} %get-tuple-element.107, f32[128,1,1536]{2,1,0:T(1,128)S(1)} %all_gather.12), kind=kOutput, calls=%fused_computation.56 | convolution fusion | flops 3023831040 | bytes 9306112 | tf_op jit(solution)/shard_map/cwt,tk->wkc/dot_general | solution.py:50
  192.3 12.5 %fusion.28 = f32[1280,128]{1,0:T(8,128)S(1)} fusion(f32[1536,640]{1,0:T(8,128)S(1)} %get-tuple-element.108, f32[1536,640]{1,0:T(8,128)S(1)} %get-tuple-element.107, f32[128,1,1536]{2,1,0:T(1,128)S(1)} %all_gather.14), kind=kOutput, calls=%fused_computation.54 | convolution fusion | flops 3023831040 | bytes 9306112 | tf_op jit(solution)/shard_map/cwt,tk->wkc/dot_general | solution.py:50
  204.9 40.9 %all-reduce.3 = (s32[64]{0:T(128)S(1)}, s32[64]{0:T(128)S(1)}) all-reduce(s32[64]{0:T(128)S(1)} %get-tuple-element.110, s32[64]{0:T(128)S(1)} %get-tuple-element.109), channel_id=1, replica_groups=mesh['row'=32,'col'=16] {'col'}, use_global_device_ids=true, to_apply=%region_1.2 | all-reduce | flops 128 | bytes 1024 | tf_op jit(solution)/shard_map/psum | solution.py:20
  245.8 1.2 fusion.90
  247.0 3.0 fusion.42
  250.2 3.0 fusion.39
  253.3 44.0 %all-reduce.7.cloned.1.call-done = (f32[64,1536]{1,0:T(8,128)}, f32[64,1536]{1,0:T(8,128)}) async-done(((f32[64,1536]{1,0:T(8,128)}, f32[64,1536]{1,0:T(8,128)}), (f32[64,1536]{1,0:T(8,128)}, f32[64,1536]{1,0:T(8,128)})) %all-reduce.7.cloned.1.call-update) | async-done | bytes 786448 | tf_op jit(solution)/shard_map/psum | solution.py:20
  297.2 8.8 %fusion.29 = f32[1280,64]{0,1:T(8,128)S(1)} fusion(f32[64,1536]{1,0:T(8,128)} %get-tuple-element.86, f32[1536,640]{1,0:T(8,128)} %copy-done.2, f32[1536,640]{1,0:T(8,128)} %copy-done), kind=kOutput, calls=%fused_computation.55 | convolution fusion | flops 1513881600 | bytes 8585216 | tf_op jit(solution)/shard_map/cwt,tk->wkc/dot_general | solution.py:50
  306.1 5.2 %fusion.31 = f32[1280,64]{0,1:T(8,128)S(1)} fusion(f32[64,1536]{1,0:T(8,128)S(1)} %copy-done.4, f32[1536,640]{1,0:T(8,128)S(1)} %copy-done.3, f32[1536,640]{1,0:T(8,128)S(1)} %copy-done.1), kind=kOutput, calls=%fused_computation.57 | convolution fusion | flops 1513881600 | bytes 8585216 | tf_op jit(solution)/shard_map/cwt,tk->wkc/dot_general | solution.py:50
  311.3 1.4 fusion.54
  312.7 1.4 fusion.48
  314.2 2.0 broadcast.137.clone
  316.2 34.9 %while.20 = (s32[]{:T(128)}, f32[4,101,16,128]{3,2,1,0:T(8,128)}, bf16[4,1280,16]{1,2,0:T(8,128)(2,1)S(1)}, bf16[1280,128]{1,0:T(8,128)(2,1)S(1)}, bf16[101,1280...) while((s32[]{:T(128)}, f32[4,101,16,128]{3,2,1,0:T(8,128)}, bf16[4,1280,16]{1,2,0:T(8,128)(2,1)S(1)}, ...), condition=%wide.region_3.4_spmd, body=%wide.region_2.3_spmd.sunk | while | flops 550686720 | bytes 27423348 | solution.py:85
  316.9 3.3 add_convert_fusion.4
  320.2 2.7 copy_bitcast_fusion.8
  322.9 1.1 fusion.132
  325.6 3.3 add_convert_fusion.4
  328.9 2.7 copy_bitcast_fusion.8
  331.6 1.1 fusion.132
  334.2 3.3 add_convert_fusion.4
  337.5 2.7 copy_bitcast_fusion.8
  340.2 1.1 fusion.132
  342.9 3.3 add_convert_fusion.4
  346.2 2.7 copy_bitcast_fusion.8
  348.9 1.1 fusion.132
  351.1 2.0 broadcast.137.clone.1
  353.1 34.7 %while.21 = (s32[]{:T(128)}, f32[4,101,16,128]{3,2,1,0:T(8,128)}, bf16[4,1280,16]{1,2,0:T(8,128)(2,1)S(1)}, bf16[1280,128]{1,0:T(8,128)(2,1)S(1)}, bf16[101,1280...) while((s32[]{:T(128)}, f32[4,101,16,128]{3,2,1,0:T(8,128)}, bf16[4,1280,16]{1,2,0:T(8,128)(2,1)S(1)}, ...), condition=%wide.region_7.8_spmd, body=%wide.region_6.7_spmd.sunk | while | flops 550686720 | bytes 27423348 | solution.py:85
  353.5 3.3 add_convert_fusion.5
  356.8 2.7 copy_bitcast_fusion.9
  359.5 1.1 fusion.136
  362.2 3.3 add_convert_fusion.5
  365.5 2.7 copy_bitcast_fusion.9
  368.2 1.1 fusion.136
  369.5 1.0 bitcast_dynamic-update-slice_fusion.7
  370.9 3.3 add_convert_fusion.5
  374.2 2.7 copy_bitcast_fusion.9
  376.9 1.1 fusion.136
  378.2 1.0 bitcast_dynamic-update-slice_fusion.7
  379.6 3.3 add_convert_fusion.5
  382.9 2.7 copy_bitcast_fusion.9
  385.6 1.1 fusion.136
  387.8 3.4 add_bitcast_fusion
  391.7 2.1 bitcast_divide_fusion
  (87 shorter events, 14.3 us)
Async XLA Ops:
  6.5 140.3 %copy-start.5 = (s32[1,4,2]{1,2,0:T(2,128)S(1)}, s32[1,4,2]{1,2,0:T(2,128)}, u32[]{:S(2)}) copy-start(s32[1,4,2]{1,2,0:T(2,128)} %param.9) | copy-start | bytes 100
  6.5 140.3 %copy-start.6 = (s32[1,4]{1,0:T(1,128)S(1)}, s32[1,4]{1,0:T(1,128)}, u32[]{:S(2)}) copy-start(s32[1,4]{1,0:T(1,128)} %param.8) | copy-start | bytes 52
  6.5 290.7 %all-reduce.7.cloned.1.call-start = ((), (), s32[]{:S(2)}) async-start(), calls=%async_computation | async-start | bytes 1572864 | tf_op jit(solution)/shard_map/psum | solution.py:20
  179.5 12.9 %copy-start = (f32[1536,640]{1,0:T(8,128)}, f32[1536,640]{1,0:T(8,128)S(1)}, u32[]{:S(2)}) copy-start(f32[1536,640]{1,0:T(8,128)S(1)} %get-tuple-element.107) | copy-start | bytes 11796484
  179.5 12.9 %copy-start.2 = (f32[1536,640]{1,0:T(8,128)}, f32[1536,640]{1,0:T(8,128)S(1)}, u32[]{:S(2)}) copy-start(f32[1536,640]{1,0:T(8,128)S(1)} %get-tuple-element.108) | copy-start | bytes 11796484
  297.2 8.8 %copy-start.1 = (f32[1536,640]{1,0:T(8,128)S(1)}, f32[1536,640]{1,0:T(8,128)}, u32[]{:S(2)}) copy-start(f32[1536,640]{1,0:T(8,128)} %copy-done) | copy-start | bytes 11796484
  297.2 8.8 %copy-start.3 = (f32[1536,640]{1,0:T(8,128)S(1)}, f32[1536,640]{1,0:T(8,128)}, u32[]{:S(2)}) copy-start(f32[1536,640]{1,0:T(8,128)} %copy-done.2) | copy-start | bytes 11796484
  297.2 8.8 %copy-start.4 = (f32[64,1536]{1,0:T(8,128)S(1)}, f32[64,1536]{1,0:T(8,128)}, u32[]{:S(2)}) copy-start(f32[64,1536]{1,0:T(8,128)} %get-tuple-element.85) | copy-start | bytes 1179652
Sparse Core Ops, SparseCore 0:
  145.0 152.2 all-reduce.6
where the time goes:
time: 409 us; the launch traced here: 401 us
  blocking collectives  192 us (47%)
  matrix products  57.3 us (14%)
  other arithmetic  50.8 us (12%)
  waiting for transfers between devices  44 us (11%)
  local copies, waits for them, and re-layouts  41.5 us (10%)
  between operations  14.7 us (4%)
    all_gather x2, blocking collectives, local(): lax.all_gather(own_series[:, window:window + 1], 'row', axis=0, tiled=True)  135 us
    psum x1, waiting for transfers between devices, broadcast(): return lax.psum(kept, axis)  44 us
    psum x1, blocking collectives, broadcast(): return lax.psum(kept, axis)  40.9 us
    dot_general x4, matrix products, whiten(): jnp.einsum('cwt,tk->wkc', series, fourier, precision=lax.Precision.HIGHEST)  39.4 us
    another operation x8, other arithmetic  26.4 us
    sub x8, local copies, waits for them, and re-layouts, correlate_group(): first_imag * partner_real - first_real * partner_imag  21.5 us
    cos x1, other arithmetic, fourier_table(): jnp.cos(phases)  16.2 us
    unnamed x1, blocking collectives  16 us
  transfers between devices with their start and end apart: 1, of which 1 were waited for; matrix products, arithmetic and copies ran while one was open for 13% of the time, Pallas kernels for 0%

commit v1 on v0

v1 whole, which is shorter than its diff:
```python
import math

import jax
import jax.numpy as jnp
import numpy as np
from jax import lax
from jax.experimental import pallas as pl
from jax.experimental.pallas import tpu as pltpu
from jax.sharding import PartitionSpec as P

NT = 1536
NF = 640
SMOOTH = 65
MAXLAG = 50
LAGS = 101
WIN = 2

LANE = 128
FOLD = NT // LANE
OWN = 4
SERIES = OWN * WIN
WIDTH = WIN * 2 * NF
SENT = WIDTH + LANE
QUICK = 4
SLOW = (LAGS + QUICK - 1) // QUICK
GROUP = 13
STEPS = SLOW // GROUP

epsilon = 1e-05


def split_high_low(values):
    high = values.astype(jnp.bfloat16)
    return high, (values - high.astype(jnp.float32)).astype(jnp.bfloat16)


def run_table():
    phases = 2.0 * np.pi * ((np.arange(LANE)[:, None] * np.arange(1, NF + 1)) % NT) / NT
    table = np.concatenate([np.cos(phases), np.sin(phases)], axis=1) / math.sqrt(NT)
    high = table.astype(jnp.bfloat16)
    low = (table - high.astype(np.float64)).astype(jnp.bfloat16)
    return high, low


def turn_table():
    phases = 2.0 * np.pi * ((np.arange(FOLD)[:, None] * np.arange(1, NF + 1)) % FOLD) / FOLD
    return np.concatenate([np.cos(phases), np.sin(phases)], axis=0).astype(np.float32)


def band_table():
    start = np.clip(np.arange(NF) - SMOOTH // 2, 0, NF - SMOOTH)
    row = np.arange(NF)[:, None]
    return ((row >= start) & (row < start + SMOOTH)).astype(jnp.bfloat16)


def lag_phases(lags):
    return 2.0 * np.pi * ((np.asarray(lags)[:, None] * np.arange(1, NF + 1)) % NT) / NT


def stride_table():
    phases = lag_phases(np.arange(SLOW) * QUICK - MAXLAG)
    return np.cos(phases).astype(np.float32), np.sin(phases).astype(np.float32)


def step_table():
    phases = lag_phases(-np.arange(QUICK))
    return np.cos(phases).astype(np.float32), np.sin(phases).astype(np.float32)


def whiten_kernel(alive_ref, keep_ref, traces_ref, high_ref, low_ref, turn_ref, band_ref, many_ref, one_ref):
    order = [(w, c) for w in range(WIN) for c in range(OWN)]
    series = jnp.concatenate([traces_ref[0, c, w : w + 1, :] for w, c in order], axis=0)
    runs = jnp.concatenate([series[:, LANE * r : LANE * (r + 1)] for r in range(FOLD)], axis=0)
    runs_high, runs_low = split_high_low(runs)
    high = high_ref[...]
    dot = lambda a, b: jnp.dot(a, b, preferred_element_type=jnp.float32)
    partial = dot(runs_high, high) + (dot(runs_low, high) + dot(runs_high, low_ref[...]))
    real = jnp.zeros((SERIES, NF), jnp.float32)
    imag = jnp.zeros((SERIES, NF), jnp.float32)
    for r in range(FOLD):
        cosine = partial[SERIES * r : SERIES * (r + 1), :NF]
        sine = partial[SERIES * r : SERIES * (r + 1), NF:]
        turn_cos, turn_sin = turn_ref[r : r + 1, :], turn_ref[FOLD + r : FOLD + r + 1, :]
        real = real + (cosine * turn_cos - sine * turn_sin)
        imag = imag - (cosine * turn_sin + sine * turn_cos)
    amplitude = jnp.sqrt(real * real + imag * imag)
    amp_high, rest = split_high_low(amplitude)[0], None
    rest = amplitude - amp_high.astype(jnp.float32)
    amp_mid, amp_low = split_high_low(rest)
    sums = dot(jnp.concatenate([amp_high, amp_mid, amp_low], axis=0), band_ref[...])
    total = sums[:SERIES] + (sums[SERIES : 2 * SERIES] + sums[2 * SERIES :])
    smooth = total * (1.0 / SMOOTH)
    row = lax.broadcasted_iota(jnp.int32, (SERIES, LANE), 0)
    weight = jnp.zeros((SERIES, LANE), jnp.float32)
    for s, (w, c) in enumerate(order):
        value = (alive_ref[0, c] * keep_ref[0, c * WIN + w]).astype(jnp.float32)
        weight = jnp.where(row == s, value, weight)
    factor = weight[:, :1] / (smooth + epsilon)
    lane = lax.broadcasted_iota(jnp.int32, (OWN, LANE), 1)
    tail = jnp.zeros((OWN, LANE), jnp.float32)
    pieces = []
    for w in range(WIN):
        rows = slice(OWN * w, OWN * (w + 1))
        pieces += [(real * factor)[rows], (imag * factor)[rows]]
        tail = jnp.where(lane == w, weight[rows], tail)
    sent = jnp.concatenate(pieces + [tail], axis=1).astype(jnp.bfloat16)
    one_ref[...] = sent
    for copy in range(many_ref.shape[0]):
        many_ref[copy] = sent


def whiten(traces, alive_mask, keep_mask, copies):
    high, low = run_table()
    vmem, smem = pl.BlockSpec(memory_space=pltpu.VMEM), pl.BlockSpec(memory_space=pltpu.SMEM)
    return pl.pallas_call(
        whiten_kernel,
        out_shape=(
            jax.ShapeDtypeStruct((copies, OWN, SENT), jnp.bfloat16),
            jax.ShapeDtypeStruct((OWN, SENT), jnp.bfloat16),
        ),
        in_specs=[smem, smem] + [vmem] * 5,
        out_specs=(vmem, vmem),
        compiler_params=pltpu.CompilerParams(vmem_limit_bytes=32 * 2**20),
        name="whiten",
    )(
        alive_mask,
        keep_mask.reshape(1, OWN * WIN),
        traces,
        jnp.asarray(high),
        jnp.asarray(low),
        jnp.asarray(turn_table()),
        jnp.asarray(band_table()),
    )


def rotate(values, cosine, sine, window):
    real = values[:, 2 * NF * window : 2 * NF * window + NF]
    imag = values[:, 2 * NF * window + NF : 2 * NF * (window + 1)]
    return real * cosine - imag * sine, real * sine + imag * cosine


def correlate_kernel(
    place_ref, first_ref, near_ref, far_ref, slow_cos, slow_sin, quick_cos, quick_sin,
    out_ref, first_wide, partner, turned, scale,
):
    rows, half = first_ref.shape[0], near_ref.shape[0]
    nt = (((1,), (1,)), ((), ()))

    @pl.when(pl.program_id(0) == 0)
    def _():
        lower = place_ref[0] == 0
        near, far = near_ref[...], far_ref[...]
        block = jnp.concatenate([jnp.where(lower, near, far), jnp.where(lower, far, near)], axis=0)
        first = first_ref[...]
        counts = lax.dot_general(first[:, WIDTH:], block[:, WIDTH:], nt, preferred_element_type=jnp.float32)
        scale[...] = (1.0 / math.sqrt(NF)) / jnp.maximum(counts, 1.0)
        first_wide[...] = first[:, :WIDTH].astype(jnp.float32)
        wide = block[:, :WIDTH].astype(jnp.float32)
        for q in range(QUICK):
            cosine, sine = quick_cos[q : q + 1, :], quick_sin[q : q + 1, :]
            for w in range(WIN):
                real, imag = rotate(wide, cosine, sine, w)
                at = slice(2 * half * q, 2 * half * (q + 1))
                partner[at, 2 * NF * w : 2 * NF * w + NF] = real.astype(jnp.bfloat16)
                partner[at, 2 * NF * w + NF : 2 * NF * (w + 1)] = imag.astype(jnp.bfloat16)

    for g in range(GROUP):
        stride = pl.program_id(0) * GROUP + g
        cosine, sine = slow_cos[pl.ds(stride, 1), :], slow_sin[pl.ds(stride, 1), :]
        at = slice(rows * g, rows * (g + 1))
        for w in range(WIN):
            real, imag = rotate(first_wide, cosine, sine, w)
            turned[at, 2 * NF * w : 2 * NF * w + NF] = real.astype(jnp.bfloat16)
            turned[at, 2 * NF * w + NF : 2 * NF * (w + 1)] = imag.astype(jnp.bfloat16)
    result = lax.dot_general(turned[...], partner[...], nt, preferred_element_type=jnp.float32)
    factor = scale[...]
    for g in range(GROUP):
        for q in range(QUICK):
            out_ref[QUICK * g + q] = (
                result[rows * g : rows * (g + 1), 2 * half * q : 2 * half * (q + 1)] * factor
            )


def correlate(place, first, near, far):
    rows, half = first.shape[0], near.shape[0]
    whole = lambda shape: pl.BlockSpec(shape, lambda i: (0,) * len(shape))
    return pl.pallas_call(
        correlate_kernel,
        grid=(STEPS,),
        out_shape=jax.ShapeDtypeStruct((LAGS, rows, 2 * half), jnp.float32),
        in_specs=[
            pl.BlockSpec(memory_space=pltpu.SMEM),
            whole((rows, SENT)),
            whole((half, SENT)),
            whole((half, SENT)),
            whole((SLOW, NF)),
            whole((SLOW, NF)),
            whole((QUICK, NF)),
            whole((QUICK, NF)),
        ],
        out_specs=pl.BlockSpec((GROUP * QUICK, rows, 2 * half), lambda i: (i, 0, 0)),
        scratch_shapes=[
            pltpu.VMEM((rows, WIDTH), jnp.float32),
            pltpu.VMEM((QUICK * 2 * half, WIDTH), jnp.bfloat16),
            pltpu.VMEM((GROUP * rows, WIDTH), jnp.bfloat16),
            pltpu.VMEM((rows, 2 * half), jnp.float32),
        ],
        compiler_params=pltpu.CompilerParams(vmem_limit_bytes=48 * 2**20),
        name="correlate",
    )(place, first, near, far, *map(jnp.asarray, stride_table() + step_table()))


def local(traces, alive_mask, keep_mask):
    row_count, col_count = lax.axis_size("row"), lax.axis_size("col")
    ring = row_count // 2
    many, own = whiten(traces, alive_mask, keep_mask, ring)
    per_row = row_count // 2
    moves = [
        (r * col_count + c, (2 * c + r // per_row) * col_count + r % per_row)
        for r in range(row_count)
        for c in range(col_count)
    ]
    mine = lax.ppermute(own, ("row", "col"), moves)
    lines = [list(range(ring)), list(range(ring, row_count))]
    near = lax.all_to_all(many, "row", 0, 0, axis_index_groups=lines).reshape(ring * OWN, SENT)
    far = lax.ppermute(near, "row", [(r, (r + ring) % row_count) for r in range(row_count)])
    shared = jnp.broadcast_to(mine[None], (col_count, OWN, SENT))
    first = lax.all_to_all(shared, "col", 0, 0).reshape(col_count * OWN, SENT)
    place = (lax.axis_index("row") // ring).astype(jnp.int32).reshape(1)
    return correlate(place, first, near, far)


def solution(mesh):
    placed = (P("col", "row", None, None), P("col", "row"), P("col", "row", None))
    return jax.shard_map(
        local, mesh=mesh, in_specs=placed, out_specs=P(None, "row", "col"), check_vma=False
    )
```

time: 409 us -> 73.9 us (0.18); the launches traced: 401 us -> 72.8 us
  blocking collectives: 192 us -> 0 us
  matrix products: 57.3 us -> 0 us
  other arithmetic: 50.8 us -> 0 us
  starting transfers between devices: 0.01 us -> 37.8 us
  local copies, waits for them, and re-layouts: 41.5 us -> 7.23 us
  waiting for transfers between devices: 44 us -> 18.2 us
  between operations: 14.7 us -> 0.09 us
  Pallas kernels: 0 us -> 9.42 us
    all_gather x2 -> x0, blocking collectives: 135 us -> none  [local(): lax.all_gather(own_series[:, window:window + 1], 'row', axis=0, tiled=True)]
    dot_general x16 -> x0, matrix products: 57.3 us -> none  [the longest x4 39.4 us: whiten(): jnp.einsum('cwt,tk->wkc', series, fourier, precision=lax.Precision.HIGHEST)]
    psum x1 -> x0, waiting for transfers between devices: 44 us -> none  [broadcast(): return lax.psum(kept, axis)]
    psum x1 -> x0, blocking collectives: 40.9 us -> none  [broadcast(): return lax.psum(kept, axis)]
    all_to_all x0 -> x2, starting transfers between devices: none -> 27.9 us  [the longest x1 15.7 us: local(): lax.all_to_all(many, 'row', 0, 0, axis_index_groups=lines)]
    another operation x8 -> x0, other arithmetic: 26.4 us -> none
    sub x8 -> x0, local copies, waits for them, and re-layouts: 21.5 us -> none  [correlate_group(): first_imag * partner_real - first_real * partner_imag]
    all_to_all x0 -> x2, waiting for transfers between devices: none -> 18.2 us  [the longest x1 10.3 us: local(): lax.all_to_all(many, 'row', 0, 0, axis_index_groups=lines)]
  transfers between devices with their start and end apart: 1 -> 4, of which waited for: 1 -> 2; matrix products, arithmetic and copies ran while one was open for 13% -> 1% of each run, Pallas kernels for 0% -> 0%
where the time goes in v1:
time: 73.9 us; the launch traced here: 72.8 us
  starting transfers between devices  37.8 us (51%)
  waiting for transfers between devices  18.2 us (25%)
  Pallas kernels  9.42 us (13%)
  local copies, waits for them, and re-layouts  7.23 us (10%)
    all_to_all x1, starting transfers between devices, local(): lax.all_to_all(many, 'row', 0, 0, axis_index_groups=lines)  15.7 us
    all_to_all x1, starting transfers between devices, local(): first = lax.all_to_all(shared, 'col', 0, 0).reshape(col_count * OWN, SENT)  12.2 us
    all_to_all x1, waiting for transfers between devices, local(): lax.all_to_all(many, 'row', 0, 0, axis_index_groups=lines)  10.3 us
    all_to_all x1, waiting for transfers between devices, local(): first = lax.all_to_all(shared, 'col', 0, 0).reshape(col_count * OWN, SENT)  7.86 us
    pallas_call x1, Pallas kernels, correlate(): pl.pallas_call(correlate_kernel, grid=(STEPS,), out_shape=jax.ShapeDtypeS...  7.47 us
    unnamed x21, local copies, waits for them, and re-layouts  6.16 us
    ppermute x1, starting transfers between devices, local(): mine = lax.ppermute(own, ('row', 'col'), moves)  5.28 us
    ppermute x1, starting transfers between devices, local(): lax.ppermute(near, 'row', [(r, (r + ring) % row_count) for r in range(row...  4.65 us
  transfers between devices with their start and end apart: 4, of which 2 were waited for; matrix products, arithmetic and copies ran while one was open for 1% of the time, Pallas kernels for 0%

profile of v1, /device:TPU:1, one launch (start us, length us, event | category | flops | bytes accessed | tf_op | source)
XLA Modules:
  0.0 72.8 jit_solution(5617927701671192824)
XLA Ops:
  0.0 0.0 copy-start.7
  0.0 0.8 %copy.13 = s32[1,4,2]{2,1,0:T(4,128)S(1)} copy(s32[1,4,2]{1,2,0:T(2,128)} %param.13) | data formatting | bytes 64 | tf_op args[2]
  0.8 0.1 reshape.14.keep_ref
  0.9 0.0 copy-start
  0.9 1.1 %copy-done = bf16[640,640]{1,0:T(8,128)(2,1)S(1)} copy-done((bf16[640,640]{1,0:T(8,128)(2,1)S(1)}, bf16[640,640]{1,0:T(8,128)(2,1)}, u32[]{:S(2)}) %copy-start) | copy-done | bytes 819224
  2.0 0.0 copy-start.1
  2.0 1.0 %copy-done.1 = bf16[128,1280]{1,0:T(8,128)(2,1)S(1)} copy-done((bf16[128,1280]{1,0:T(8,128)(2,1)S(1)}, bf16[128,1280]{1,0:T(8,128)(2,1)}, u32[]{:S(2)}) %copy-start.1) | copy-done | bytes 327704
  3.0 0.0 copy-start.2
  3.0 1.0 %copy-done.2 = bf16[128,1280]{1,0:T(8,128)(2,1)S(1)} copy-done((bf16[128,1280]{1,0:T(8,128)(2,1)S(1)}, bf16[128,1280]{1,0:T(8,128)(2,1)}, u32[]{:S(2)}) %copy-start.2) | copy-done | bytes 327704
  4.0 0.0 copy-start.5
  4.0 0.8 %copy-done.5 = f32[24,640]{1,0:T(8,128)S(1)} copy-done((f32[24,640]{1,0:T(8,128)S(1)}, f32[24,640]{1,0:T(8,128)}, u32[]{:S(2)}) %copy-start.5) | copy-done | bytes 61464
  4.8 0.0 copy-start.6
  4.8 0.8 %copy-done.6 = f32[1,4,2,1536]{3,2,1,0:T(2,128)S(1)} copy-done((f32[1,4,2,1536]{3,2,1,0:T(2,128)S(1)}, f32[1,4,2,1536]{3,2,1,0:T(2,128)}, u32[]{:S(2)}) %copy-start.6) | copy-done | bytes 49176
  5.6 0.0 copy-start.9
  5.6 0.7 copy-done.9
  6.2 0.0 copy-start.3
  6.2 0.0 copy-start.4
  6.2 0.0 copy-start.8
  6.2 2.0 %whiten.1 = (bf16[16,4,2688]{2,1,0:T(4,128)(2,1)}, bf16[4,2688]{1,0:T(4,128)(2,1)S(1)}) custom-call(s32[1,4]{1,0:T(1,128)S(1)} %copy-done.9, s32[1,8]{1,0:T(1,128)S(1)} %reshape.14.keep_ref, f32[1,4,2,1536]{3,2,1,0:T(2,128)S(1)} %copy-done.6, bf16[128,1280]{1,0:T(8,128)(2,1)S(1)} %copy-done.2, bf16[128,1280]{1,0:T(8,128)(2,1)S(1)} %copy-done.1, ...), custom_call_target="tpu_custom_call" | custom-call | tf_op jit(solution)/shard_map/whiten/pallas_call | solution.py:115
  8.2 15.7 %all-to-all-start.1 = ((bf16[16,4,2688]{2,1,0:T(4,128)(2,1)}), bf16[16,4,2688]{2,1,0:T(4,128)(2,1)S(1)}, u32[]{:S(2)}, u32[]{:S(2)}) async-start(bf16[16,4,2688]{2,1,0:T(4,128)(2,1)} %get-tuple-element.8), calls=%async_computation.1 | async-start | bytes 688128 | tf_op jit(solution)/shard_map/all_to_all | solution.py:225
  24.0 5.3 %collective-permute-start = (bf16[4,2688]{1,0:T(4,128)(2,1)S(1)}, bf16[4,2688]{1,0:T(4,128)(2,1)S(1)}, u32[]{:S(2)}, u32[]{:S(2)}) collective-permute-start(bf16[4,2688]{1,0:T(4,128)(2,1)S(1)} %get-tuple-element.7), channel_id=1, source_target_pairs={{0,0},{1,32},{2,64},{3,96},{4,128},{5,160},{6,192},{7,224},{8,256}... | collective-permute-start | bytes 64520 | tf_op jit(solution)/shard_map/ppermute | solution.py:223
  29.2 10.3 %all-to-all-done.1 = bf16[16,4,2688]{2,1,0:T(4,128)(2,1)S(1)} async-done(((bf16[16,4,2688]{2,1,0:T(4,128)(2,1)}), bf16[16,4,2688]{2,1,0:T(4,128)(2,1)S(1)}, u32[]{:S(2)}, u32[]{:S(2)}) %all-to-all-start.1) | async-done | bytes 344096 | tf_op jit(solution)/shard_map/all_to_all | solution.py:225
  39.6 0.1 reshape.16.near_ref
  39.7 4.7 %collective-permute-start.1 = (bf16[64,2688]{1,0:T(8,128)(2,1)S(1)}, bf16[64,2688]{1,0:T(8,128)(2,1)S(1)}, u32[]{:S(2)}, u32[]{:S(2)}) collective-permute-start(bf16[64,2688]{1,0:T(8,128)(2,1)S(1)} %reshape.16.near_ref), channel_id=1, source_target_pairs={{0,256},{16,272},{32,288},{48,304},{64,320},{80,336},{96,352},{112... | collective-permute-start | bytes 1032200 | tf_op jit(solution)/shard_map/ppermute | solution.py:226
  44.3 0.0 collective-permute-done
  44.3 0.8 %broadcast_in_dim.2 = bf16[16,4,2688]{2,1,0:T(4,128)(2,1)} broadcast(bf16[4,2688]{1,0:T(4,128)(2,1)S(1)} %collective-permute-done), dimensions={1,2} | broadcast | bytes 365568 | tf_op jit(solution)/shard_map/broadcast_in_dim | solution.py:227
  45.2 12.2 %all-to-all-start = ((bf16[16,4,2688]{2,1,0:T(4,128)(2,1)}), bf16[16,4,2688]{2,1,0:T(4,128)(2,1)S(1)}, u32[]{:S(2)}, u32[]{:S(2)}) async-start(bf16[16,4,2688]{2,1,0:T(4,128)(2,1)} %broadcast_in_dim.2), calls=%async_computation | async-start | bytes 688128 | tf_op jit(solution)/shard_map/all_to_all | solution.py:228
  57.3 7.9 %all-to-all-done = bf16[16,4,2688]{2,1,0:T(4,128)(2,1)S(1)} async-done(((bf16[16,4,2688]{2,1,0:T(4,128)(2,1)}), bf16[16,4,2688]{2,1,0:T(4,128)(2,1)S(1)}, u32[]{:S(2)}, u32[]{:S(2)}) %all-to-all-start) | async-done | bytes 344096 | tf_op jit(solution)/shard_map/all_to_all | solution.py:228
  65.2 0.1 reshape.15.first_ref
  65.3 0.0 collective-permute-done.1.far_ref
  65.3 0.0 copy-done.7
  65.3 0.0 copy-done.3
  65.3 0.0 copy-done.4
  65.3 0.0 copy-done.8
  65.3 7.5 %correlate.1 = f32[101,64,128]{2,1,0:T(8,128)} custom-call(s32[1]{0:T(128)} %bitcast.place_ref, bf16[64,2688]{1,0:T(8,128)(2,1)S(1)} %reshape.15.first_ref, bf16[64,2688]{1,0:T(8,128)(2,1)S(1)} %reshape.16.near_ref, bf16[64,2688]{1,0:T(8,128)(2,1)S(1)} %collective-permute-done.1.far_ref, f32[26,640]{1,0:T(8,128)S(1)} %copy-done.4, f32[26,640]{1,0:T(8,128)S(1)} %copy-done.3, ...), custom_call_target="tpu_custom_call" | custom-call | tf_op jit(solution)/shard_map/correlate/pallas_call | solution.py:187
Async XLA Ops:
  0.0 65.3 %copy-start.7 = (f32[4,640]{1,0:T(4,128)S(1)}, f32[4,640]{1,0:T(4,128)}, u32[]{:S(2)}) copy-start(f32[4,640]{1,0:T(4,128)} %constant.45.clone.quick_sin) | copy-start | bytes 30724
  0.9 1.1 %copy-start = (bf16[640,640]{1,0:T(8,128)(2,1)S(1)}, bf16[640,640]{1,0:T(8,128)(2,1)}, u32[]{:S(2)}) copy-start(bf16[640,640]{1,0:T(8,128)(2,1)} %constant.41.clone.band_ref) | copy-start | bytes 2457604
  2.0 1.0 %copy-start.1 = (bf16[128,1280]{1,0:T(8,128)(2,1)S(1)}, bf16[128,1280]{1,0:T(8,128)(2,1)}, u32[]{:S(2)}) copy-start(bf16[128,1280]{1,0:T(8,128)(2,1)} %constant.39.clone.low_ref) | copy-start | bytes 983044
  3.0 1.0 %copy-start.2 = (bf16[128,1280]{1,0:T(8,128)(2,1)S(1)}, bf16[128,1280]{1,0:T(8,128)(2,1)}, u32[]{:S(2)}) copy-start(bf16[128,1280]{1,0:T(8,128)(2,1)} %constant.38.clone.high_ref) | copy-start | bytes 983044
  4.0 0.8 %copy-start.5 = (f32[24,640]{1,0:T(8,128)S(1)}, f32[24,640]{1,0:T(8,128)}, u32[]{:S(2)}) copy-start(f32[24,640]{1,0:T(8,128)} %constant.40.clone.turn_ref) | copy-start | bytes 184324
  4.8 0.8 %copy-start.6 = (f32[1,4,2,1536]{3,2,1,0:T(2,128)S(1)}, f32[1,4,2,1536]{3,2,1,0:T(2,128)}, u32[]{:S(2)}) copy-start(f32[1,4,2,1536]{3,2,1,0:T(2,128)} %traces_ref.1) | copy-start | bytes 147460
  5.6 0.7 copy-start.9
  6.2 59.0 %copy-start.3 = (f32[26,640]{1,0:T(8,128)S(1)}, f32[26,640]{1,0:T(8,128)}, u32[]{:S(2)}) copy-start(f32[26,640]{1,0:T(8,128)} %constant.43.clone.slow_sin) | copy-start | bytes 199684
  6.2 59.0 %copy-start.4 = (f32[26,640]{1,0:T(8,128)S(1)}, f32[26,640]{1,0:T(8,128)}, u32[]{:S(2)}) copy-start(f32[26,640]{1,0:T(8,128)} %constant.42.clone.slow_cos) | copy-start | bytes 199684
  6.2 59.1 %copy-start.8 = (f32[4,640]{1,0:T(4,128)S(1)}, f32[4,640]{1,0:T(4,128)}, u32[]{:S(2)}) copy-start(f32[4,640]{1,0:T(4,128)} %constant.44.clone.quick_cos) | copy-start | bytes 30724
  8.2 31.4 %all-to-all-start.1 = ((bf16[16,4,2688]{2,1,0:T(4,128)(2,1)}), bf16[16,4,2688]{2,1,0:T(4,128)(2,1)S(1)}, u32[]{:S(2)}, u32[]{:S(2)}) async-start(bf16[16,4,2688]{2,1,0:T(4,128)(2,1)} %get-tuple-element.8), calls=%async_computation.1 | async-start | bytes 688128 | tf_op jit(solution)/shard_map/all_to_all | solution.py:225
  24.0 20.4 %collective-permute-start = (bf16[4,2688]{1,0:T(4,128)(2,1)S(1)}, bf16[4,2688]{1,0:T(4,128)(2,1)S(1)}, u32[]{:S(2)}, u32[]{:S(2)}) collective-permute-start(bf16[4,2688]{1,0:T(4,128)(2,1)S(1)} %get-tuple-element.7), channel_id=1, source_target_pairs={{0,0},{1,32},{2,64},{3,96},{4,128},{5,160},{6,192},{7,224},{8,256}... | collective-permute-start | bytes 64520 | tf_op jit(solution)/shard_map/ppermute | solution.py:223
  39.7 25.6 %collective-permute-start.1 = (bf16[64,2688]{1,0:T(8,128)(2,1)S(1)}, bf16[64,2688]{1,0:T(8,128)(2,1)S(1)}, u32[]{:S(2)}, u32[]{:S(2)}) collective-permute-start(bf16[64,2688]{1,0:T(8,128)(2,1)S(1)} %reshape.16.near_ref), channel_id=1, source_target_pairs={{0,256},{16,272},{32,288},{48,304},{64,320},{80,336},{96,352},{112... | collective-permute-start | bytes 1032200 | tf_op jit(solution)/shard_map/ppermute | solution.py:226
  45.2 20.0 %all-to-all-start = ((bf16[16,4,2688]{2,1,0:T(4,128)(2,1)}), bf16[16,4,2688]{2,1,0:T(4,128)(2,1)S(1)}, u32[]{:S(2)}, u32[]{:S(2)}) async-start(bf16[16,4,2688]{2,1,0:T(4,128)(2,1)} %broadcast_in_dim.2), calls=%async_computation | async-start | bytes 688128 | tf_op jit(solution)/shard_map/all_to_all | solution.py:228

commit v2 on v1

v2 whole, which is shorter than its diff:
```python
import math

import jax
import jax.numpy as jnp
import numpy as np
from jax import lax
from jax.experimental import pallas as pl
from jax.experimental.pallas import tpu as pltpu
from jax.sharding import PartitionSpec as P

NT = 1536
NF = 640
SMOOTH = 65
MAXLAG = 50
LAGS = 101
WIN = 2

LANE = 128
FOLD = NT // LANE
OWN = 4
SERIES = OWN * WIN
WIDTH = WIN * 2 * NF
SENT = WIDTH + LANE
QUICK = 4
SLOW = (LAGS + QUICK - 1) // QUICK
GROUP = 13
STEPS = SLOW // GROUP

epsilon = 1e-05


def split_high_low(values):
    high = values.astype(jnp.bfloat16)
    return high, (values - high.astype(jnp.float32)).astype(jnp.bfloat16)


def run_table():
    phases = 2.0 * np.pi * ((np.arange(LANE)[:, None] * np.arange(1, NF + 1)) % NT) / NT
    table = np.concatenate([np.cos(phases), np.sin(phases)], axis=1) / math.sqrt(NT)
    high = table.astype(jnp.bfloat16)
    low = (table - high.astype(np.float64)).astype(jnp.bfloat16)
    return high, low


def turn_table():
    phases = 2.0 * np.pi * ((np.arange(FOLD)[:, None] * np.arange(1, NF + 1)) % FOLD) / FOLD
    return np.concatenate([np.cos(phases), np.sin(phases)], axis=0).astype(np.float32)


def band_table():
    start = np.clip(np.arange(NF) - SMOOTH // 2, 0, NF - SMOOTH)
    row = np.arange(NF)[:, None]
    return ((row >= start) & (row < start + SMOOTH)).astype(jnp.bfloat16)


def lag_phases(lags):
    return 2.0 * np.pi * ((np.asarray(lags)[:, None] * np.arange(1, NF + 1)) % NT) / NT


def stride_table():
    phases = lag_phases(np.arange(SLOW) * QUICK - MAXLAG)
    return np.cos(phases).astype(np.float32), np.sin(phases).astype(np.float32)


def step_table():
    phases = lag_phases(-np.arange(QUICK))
    return np.cos(phases).astype(np.float32), np.sin(phases).astype(np.float32)


def whiten_kernel(
    alive_hbm, keep_hbm, traces_hbm, high_hbm, low_hbm, turn_hbm, band_hbm, many_ref, one_ref,
    alive_ref, keep_ref, traces_ref, high_ref, low_ref, turn_ref, band_ref, arrived,
):
    sources = (traces_hbm, high_hbm, low_hbm, turn_hbm, alive_hbm, keep_hbm, band_hbm)
    targets = (traces_ref, high_ref, low_ref, turn_ref, alive_ref, keep_ref, band_ref)
    copies = [
        pltpu.make_async_copy(source, target, arrived.at[n])
        for n, (source, target) in enumerate(zip(sources, targets, strict=True))
    ]
    for copy in copies:
        copy.start()
    order = [(w, c) for w in range(WIN) for c in range(OWN)]
    dot = lambda a, b: jnp.dot(a, b, preferred_element_type=jnp.float32)
    for copy in copies[:4]:
        copy.wait()
    series = jnp.concatenate([traces_ref[0, c, w : w + 1, :] for w, c in order], axis=0)
    runs = jnp.concatenate([series[:, LANE * r : LANE * (r + 1)] for r in range(FOLD)], axis=0)
    runs_high, runs_low = split_high_low(runs)
    high = high_ref[...]
    partial = dot(runs_high, high) + (dot(runs_low, high) + dot(runs_high, low_ref[...]))
    real = jnp.zeros((SERIES, NF), jnp.float32)
    imag = jnp.zeros((SERIES, NF), jnp.float32)
    for r in range(FOLD):
        cosine = partial[SERIES * r : SERIES * (r + 1), :NF]
        sine = partial[SERIES * r : SERIES * (r + 1), NF:]
        turn_cos, turn_sin = turn_ref[r : r + 1, :], turn_ref[FOLD + r : FOLD + r + 1, :]
        real = real + (cosine * turn_cos - sine * turn_sin)
        imag = imag - (cosine * turn_sin + sine * turn_cos)
    amplitude = jnp.sqrt(real * real + imag * imag)
    amp_high = amplitude.astype(jnp.bfloat16)
    amp_mid, amp_low = split_high_low(amplitude - amp_high.astype(jnp.float32))
    for copy in copies[4:]:
        copy.wait()
    sums = dot(jnp.concatenate([amp_high, amp_mid, amp_low], axis=0), band_ref[...])
    total = sums[:SERIES] + (sums[SERIES : 2 * SERIES] + sums[2 * SERIES :])
    smooth = total * (1.0 / SMOOTH)
    row = lax.broadcasted_iota(jnp.int32, (SERIES, LANE), 0)
    weight = jnp.zeros((SERIES, LANE), jnp.float32)
    for s, (w, c) in enumerate(order):
        value = (alive_ref[0, c] * keep_ref[0, w, c]).astype(jnp.float32)
        weight = jnp.where(row == s, value, weight)
    factor = weight[:, :1] / (smooth + epsilon)
    lane = lax.broadcasted_iota(jnp.int32, (OWN, LANE), 1)
    tail = jnp.zeros((OWN, LANE), jnp.float32)
    pieces = []
    for w in range(WIN):
        rows = slice(OWN * w, OWN * (w + 1))
        pieces += [(real * factor)[rows], (imag * factor)[rows]]
        tail = jnp.where(lane == w, weight[rows], tail)
    sent = jnp.concatenate(pieces + [tail], axis=1).astype(jnp.bfloat16)
    one_ref[...] = sent
    for copy in range(many_ref.shape[0]):
        many_ref[copy] = sent


def whiten(traces, alive, keep, copies):
    high, low = run_table()
    shapes = [(1, OWN, WIN, NT), high.shape, low.shape, (2 * FOLD, NF), (NF, NF)]
    dtypes = [jnp.float32, jnp.bfloat16, jnp.bfloat16, jnp.float32, jnp.bfloat16]
    return pl.pallas_call(
        whiten_kernel,
        out_shape=(
            jax.ShapeDtypeStruct((copies, OWN, SENT), jnp.bfloat16),
            jax.ShapeDtypeStruct((OWN, SENT), jnp.bfloat16),
        ),
        in_specs=[pl.BlockSpec(memory_space=pltpu.HBM)] * 7,
        out_specs=(pl.BlockSpec(memory_space=pltpu.VMEM),) * 2,
        scratch_shapes=[pltpu.SMEM((1, OWN), jnp.int32), pltpu.SMEM((1, WIN, OWN), jnp.int32)]
        + [pltpu.VMEM(shape, dtype) for shape, dtype in zip(shapes, dtypes, strict=True)]
        + [pltpu.SemaphoreType.DMA((7,))],
        compiler_params=pltpu.CompilerParams(vmem_limit_bytes=60 * 2**20),
        name="whiten",
    )(
        alive,
        keep,
        traces,
        jnp.asarray(high),
        jnp.asarray(low),
        jnp.asarray(turn_table()),
        jnp.asarray(band_table()),
    )


def rotate(values, cosine, sine, window):
    real = values[:, 2 * NF * window : 2 * NF * window + NF]
    imag = values[:, 2 * NF * window + NF : 2 * NF * (window + 1)]
    return real * cosine - imag * sine, real * sine + imag * cosine


def partner_kernel(place_ref, near_ref, far_ref, quick_cos, quick_sin, turned_ref, weight_ref):
    lower = place_ref[0] == 0
    near, far = near_ref[...], far_ref[...]
    block = jnp.concatenate([jnp.where(lower, near, far), jnp.where(lower, far, near)], axis=0)
    weight_ref[...] = block[:, WIDTH:]
    wide = block[:, :WIDTH].astype(jnp.float32)
    for q in range(QUICK):
        cosine, sine = quick_cos[q : q + 1, :], quick_sin[q : q + 1, :]
        at = slice(LANE * q, LANE * (q + 1))
        for w in range(WIN):
            for part, value in enumerate(rotate(wide, cosine, sine, w)):
                start = NF * (WIN * w + part)
                turned_ref[start : start + NF, at] = jnp.transpose(value).astype(jnp.bfloat16)


def turn_partner(place, near, far):
    vmem = pl.BlockSpec(memory_space=pltpu.VMEM)
    return pl.pallas_call(
        partner_kernel,
        out_shape=(
            jax.ShapeDtypeStruct((WIDTH, QUICK * LANE), jnp.bfloat16),
            jax.ShapeDtypeStruct((LANE, LANE), jnp.bfloat16),
        ),
        in_specs=[pl.BlockSpec(memory_space=pltpu.SMEM)] + [vmem] * 4,
        out_specs=(vmem, vmem),
        compiler_params=pltpu.CompilerParams(vmem_limit_bytes=32 * 2**20),
        cost_estimate=pl.CostEstimate(flops=2 * 10**10, bytes_accessed=5 * 10**6, transcendentals=0),
        name="turn_partner",
    )(place, near, far, *map(jnp.asarray, step_table()))


def correlate_kernel(first_ref, partner_ref, weight_ref, slow_cos, slow_sin, out_ref, first_wide, turned, scale):
    rows = first_ref.shape[0]

    @pl.when(pl.program_id(0) == 0)
    def _():
        first = first_ref[...]
        counts = lax.dot_general(
            first[:, WIDTH:], weight_ref[...], (((1,), (1,)), ((), ())), preferred_element_type=jnp.float32
        )
        scale[...] = (1.0 / math.sqrt(NF)) / jnp.maximum(counts, 1.0)
        first_wide[...] = first[:, :WIDTH].astype(jnp.float32)

    for g in range(GROUP):
        stride = pl.program_id(0) * GROUP + g
        cosine, sine = slow_cos[pl.ds(stride, 1), :], slow_sin[pl.ds(stride, 1), :]
        at = slice(rows * g, rows * (g + 1))
        for w in range(WIN):
            for part, value in enumerate(rotate(first_wide, cosine, sine, w)):
                start = NF * (WIN * w + part)
                turned[at, start : start + NF] = value.astype(jnp.bfloat16)
    result = jnp.dot(turned[...], partner_ref[...], preferred_element_type=jnp.float32)
    factor = scale[...]
    for g in range(GROUP):
        for q in range(QUICK):
            out_ref[QUICK * g + q] = (
                result[rows * g : rows * (g + 1), LANE * q : LANE * (q + 1)] * factor
            )


def correlate(first, partner, weight):
    rows = first.shape[0]
    whole = lambda shape: pl.BlockSpec(shape, lambda i: (0,) * len(shape))
    return pl.pallas_call(
        correlate_kernel,
        grid=(STEPS,),
        out_shape=jax.ShapeDtypeStruct((LAGS, rows, LANE), jnp.float32),
        in_specs=[
            whole((rows, SENT)),
            whole(partner.shape),
            whole(weight.shape),
            whole((SLOW, NF)),
            whole((SLOW, NF)),
        ],
        out_specs=pl.BlockSpec((GROUP * QUICK, rows, LANE), lambda i: (i, 0, 0)),
        scratch_shapes=[
            pltpu.VMEM((rows, WIDTH), jnp.float32),
            pltpu.VMEM((GROUP * rows, WIDTH), jnp.bfloat16),
            pltpu.VMEM((rows, LANE), jnp.float32),
        ],
        compiler_params=pltpu.CompilerParams(vmem_limit_bytes=36 * 2**20),
        name="correlate",
    )(first, partner, weight, *map(jnp.asarray, stride_table()))


def local(traces, alive_mask, keep_mask):
    row_count, col_count = lax.axis_size("row"), lax.axis_size("col")
    ring = row_count // 2
    place = (lax.axis_index("row") // ring).astype(jnp.int32).reshape(1)
    many, own = whiten(traces, alive_mask, jnp.transpose(keep_mask, (0, 2, 1)), ring)
    moves = [
        (r * col_count + c, (2 * c + r // ring) * col_count + r % ring)
        for r in range(row_count)
        for c in range(col_count)
    ]
    mine = lax.ppermute(own, ("row", "col"), moves)
    lines = [list(range(ring)), list(range(ring, row_count))]
    near = lax.all_to_all(many, "row", 0, 0, axis_index_groups=lines).reshape(ring * OWN, SENT)
    far = lax.ppermute(near, "row", [(r, (r + ring) % row_count) for r in range(row_count)])
    shared = jnp.broadcast_to(mine[None], (col_count, OWN, SENT))
    first = lax.all_to_all(shared, "col", 0, 0).reshape(col_count * OWN, SENT)
    partner, weight = turn_partner(place, near, far)
    return correlate(first, partner, weight)


def solution(mesh):
    placed = (P("col", "row", None, None), P("col", "row"), P("col", "row", None))
    return jax.shard_map(
        local, mesh=mesh, in_specs=placed, out_specs=P(None, "row", "col"), check_vma=False
    )
```

time: 73.9 us -> 68 us (0.920)
  local copies, waits for them, and re-layouts: 7.23 us -> 1.01 us
    unnamed x21 -> x8, local copies, waits for them, and re-layouts: 6.16 us -> 0.02 us
    pallas_call x1, Pallas kernels: 7.47 us -> 6.12 us  [correlate(): pl.pallas_call(correlate_kernel, grid=(STEPS,), out_shape=jax.ShapeDtypeS...]
    pallas_call x0 -> x1, Pallas kernels: none -> 1.09 us  [turn_partner(): pl.pallas_call(partner_kernel, out_shape=(jax.ShapeDtypeStruct((WIDTH, QU...]
where the time goes in v2:
time: 68 us; the launch traced here: 67 us
  starting transfers between devices  37.8 us (56%)
  waiting for transfers between devices  18.2 us (27%)
  Pallas kernels  9.88 us (15%)
  local copies, waits for them, and re-layouts  1.01 us (1%)
    all_to_all x1, starting transfers between devices, local(): lax.all_to_all(many, 'row', 0, 0, axis_index_groups=lines)  15.8 us
    all_to_all x1, starting transfers between devices, local(): first = lax.all_to_all(shared, 'col', 0, 0).reshape(col_count * OWN, SENT)  12.2 us
    all_to_all x1, waiting for transfers between devices, local(): lax.all_to_all(many, 'row', 0, 0, axis_index_groups=lines)  10.3 us
    all_to_all x1, waiting for transfers between devices, local(): first = lax.all_to_all(shared, 'col', 0, 0).reshape(col_count * OWN, SENT)  7.86 us
    pallas_call x1, Pallas kernels, correlate(): pl.pallas_call(correlate_kernel, grid=(STEPS,), out_shape=jax.ShapeDtypeS...  6.12 us
    ppermute x1, starting transfers between devices, local(): mine = lax.ppermute(own, ('row', 'col'), moves)  5.28 us
    ppermute x1, starting transfers between devices, local(): lax.ppermute(near, 'row', [(r, (r + ring) % row_count) for r in range(row...  4.65 us
    pallas_call x1, Pallas kernels, whiten(): pl.pallas_call(whiten_kernel, out_shape=(jax.ShapeDtypeStruct((copies, OW...  2.67 us
  transfers between devices with their start and end apart: 4, of which 2 were waited for; matrix products, arithmetic and copies ran while one was open for 1% of the time, Pallas kernels for 0%

profile of v2, /device:TPU:1, one launch (start us, length us, event | category | flops | bytes accessed | tf_op | source)
XLA Modules:
  0.0 67.0 jit_solution(12879344123152537109)
XLA Ops:
  0.0 0.0 copy-start.2
  0.0 0.0 copy-start.3
  0.0 2.7 %whiten.1 = (bf16[16,4,2688]{2,1,0:T(4,128)(2,1)}, bf16[4,2688]{1,0:T(4,128)(2,1)}) custom-call(s32[1,4]{1,0:T(1,128)} %alive_hbm.1, s32[1,2,4]{2,1,0:T(2,128)} %bitcast.2, f32[1,4,2,1536]{3,2,1,0:T(2,128)} %traces_hbm.1, bf16[128,1280]{1,0:T(8,128)(2,1)} %constant.38.clone.high_hbm, bf16[128,1280]{1,0:T(8,128)(2,1)} %constant.39.clone.low_hbm, ...), custom_call_target="tpu_custom_call" | custom-call | tf_op jit(solution)/shard_map/whiten/pallas_call | solution.py:130
  2.7 15.8 %all-to-all-start.1 = ((bf16[16,4,2688]{2,1,0:T(4,128)(2,1)}), bf16[16,4,2688]{2,1,0:T(4,128)(2,1)S(1)}, u32[]{:S(2)}, u32[]{:S(2)}) async-start(bf16[16,4,2688]{2,1,0:T(4,128)(2,1)} %get-tuple-element.10), calls=%async_computation.1 | async-start | bytes 688128 | tf_op jit(solution)/shard_map/all_to_all | solution.py:257
  18.4 5.3 %collective-permute-start = (bf16[4,2688]{1,0:T(4,128)(2,1)}, bf16[4,2688]{1,0:T(4,128)(2,1)S(1)}, u32[]{:S(2)}, u32[]{:S(2)}) collective-permute-start(bf16[4,2688]{1,0:T(4,128)(2,1)} %get-tuple-element.9), channel_id=1, source_target_pairs={{0,0},{1,32},{2,64},{3,96},{4,128},{5,160},{6,192},{7,224},{8,256}... | collective-permute-start | bytes 64520 | tf_op jit(solution)/shard_map/ppermute | solution.py:255
  23.7 10.3 %all-to-all-done.1 = bf16[16,4,2688]{2,1,0:T(4,128)(2,1)S(1)} async-done(((bf16[16,4,2688]{2,1,0:T(4,128)(2,1)}), bf16[16,4,2688]{2,1,0:T(4,128)(2,1)S(1)}, u32[]{:S(2)}, u32[]{:S(2)}) %all-to-all-start.1) | async-done | bytes 344096 | tf_op jit(solution)/shard_map/all_to_all | solution.py:257
  34.1 0.1 reshape.12.near_ref
  34.2 4.7 %collective-permute-start.1 = (bf16[64,2688]{1,0:T(8,128)(2,1)S(1)}, bf16[64,2688]{1,0:T(8,128)(2,1)S(1)}, u32[]{:S(2)}, u32[]{:S(2)}) collective-permute-start(bf16[64,2688]{1,0:T(8,128)(2,1)S(1)} %reshape.12.near_ref), channel_id=1, source_target_pairs={{0,256},{16,272},{32,288},{48,304},{64,320},{80,336},{96,352},{112... | collective-permute-start | bytes 1032200 | tf_op jit(solution)/shard_map/ppermute | solution.py:258
  38.8 0.0 collective-permute-done
  38.8 0.8 %broadcast_in_dim.2 = bf16[16,4,2688]{2,1,0:T(4,128)(2,1)} broadcast(bf16[4,2688]{1,0:T(4,128)(2,1)S(1)} %collective-permute-done), dimensions={1,2} | broadcast | bytes 365568 | tf_op jit(solution)/shard_map/broadcast_in_dim | solution.py:259
  39.6 12.2 %all-to-all-start = ((bf16[16,4,2688]{2,1,0:T(4,128)(2,1)}), bf16[16,4,2688]{2,1,0:T(4,128)(2,1)S(1)}, u32[]{:S(2)}, u32[]{:S(2)}) async-start(bf16[16,4,2688]{2,1,0:T(4,128)(2,1)} %broadcast_in_dim.2), calls=%async_computation | async-start | bytes 688128 | tf_op jit(solution)/shard_map/all_to_all | solution.py:260
  51.8 7.9 %all-to-all-done = bf16[16,4,2688]{2,1,0:T(4,128)(2,1)S(1)} async-done(((bf16[16,4,2688]{2,1,0:T(4,128)(2,1)}), bf16[16,4,2688]{2,1,0:T(4,128)(2,1)S(1)}, u32[]{:S(2)}, u32[]{:S(2)}) %all-to-all-start) | async-done | bytes 344096 | tf_op jit(solution)/shard_map/all_to_all | solution.py:260
  59.7 0.1 reshape.10.first_ref
  59.7 0.0 collective-permute-done.1.far_ref
  59.8 0.0 copy-done.2
  59.8 0.0 copy-done.3
  59.8 0.0 copy-start
  59.8 0.0 copy-start.1
  59.8 1.1 %turn_partner.1 = (bf16[2560,512]{1,0:T(8,128)(2,1)S(1)}, bf16[128,128]{1,0:T(8,128)(2,1)S(1)}) custom-call(s32[1]{0:T(128)} %bitcast.1.place_ref, bf16[64,2688]{1,0:T(8,128)(2,1)S(1)} %reshape.12.near_ref, bf16[64,2688]{1,0:T(8,128)(2,1)S(1)} %collective-permute-done.1.far_ref, f32[4,640]{1,0:T(4,128)S(1)} %copy-done.3, f32[4,640]{1,0:T(4,128)S(1)} %copy-done.2), custom_call_target="tpu_custom_call" | custom-call | flops 20000000000 | bytes 5000000 | tf_op jit(solution)/shard_map/turn_partner/pallas_call | solution.py:177
  60.9 0.0 copy-done
  60.9 0.0 copy-done.1
  60.9 6.1 %correlate.1 = f32[101,64,128]{2,1,0:T(8,128)} custom-call(bf16[64,2688]{1,0:T(8,128)(2,1)S(1)} %reshape.10.first_ref, bf16[2560,512]{1,0:T(8,128)(2,1)S(1)} %get-tuple-element.11.partner_ref, bf16[128,128]{1,0:T(8,128)(2,1)S(1)} %get-tuple-element.12.weight_ref, f32[26,640]{1,0:T(8,128)S(1)} %copy-done.1, f32[26,640]{1,0:T(8,128)S(1)} %copy-done), custom_call_target="tpu_custom_call" | custom-call | tf_op jit(solution)/shard_map/correlate/pallas_call | solution.py:223
Async XLA Ops:
  0.0 59.8 %copy-start.2 = (f32[4,640]{1,0:T(4,128)S(1)}, f32[4,640]{1,0:T(4,128)}, u32[]{:S(2)}) copy-start(f32[4,640]{1,0:T(4,128)} %constant.43.clone.quick_sin) | copy-start | bytes 30724
  0.0 59.8 %copy-start.3 = (f32[4,640]{1,0:T(4,128)S(1)}, f32[4,640]{1,0:T(4,128)}, u32[]{:S(2)}) copy-start(f32[4,640]{1,0:T(4,128)} %constant.42.clone.quick_cos) | copy-start | bytes 30724
  2.7 31.4 %all-to-all-start.1 = ((bf16[16,4,2688]{2,1,0:T(4,128)(2,1)}), bf16[16,4,2688]{2,1,0:T(4,128)(2,1)S(1)}, u32[]{:S(2)}, u32[]{:S(2)}) async-start(bf16[16,4,2688]{2,1,0:T(4,128)(2,1)} %get-tuple-element.10), calls=%async_computation.1 | async-start | bytes 688128 | tf_op jit(solution)/shard_map/all_to_all | solution.py:257
  18.4 20.4 %collective-permute-start = (bf16[4,2688]{1,0:T(4,128)(2,1)}, bf16[4,2688]{1,0:T(4,128)(2,1)S(1)}, u32[]{:S(2)}, u32[]{:S(2)}) collective-permute-start(bf16[4,2688]{1,0:T(4,128)(2,1)} %get-tuple-element.9), channel_id=1, source_target_pairs={{0,0},{1,32},{2,64},{3,96},{4,128},{5,160},{6,192},{7,224},{8,256}... | collective-permute-start | bytes 64520 | tf_op jit(solution)/shard_map/ppermute | solution.py:255
  34.2 25.6 %collective-permute-start.1 = (bf16[64,2688]{1,0:T(8,128)(2,1)S(1)}, bf16[64,2688]{1,0:T(8,128)(2,1)S(1)}, u32[]{:S(2)}, u32[]{:S(2)}) collective-permute-start(bf16[64,2688]{1,0:T(8,128)(2,1)S(1)} %reshape.12.near_ref), channel_id=1, source_target_pairs={{0,256},{16,272},{32,288},{48,304},{64,320},{80,336},{96,352},{112... | collective-permute-start | bytes 1032200 | tf_op jit(solution)/shard_map/ppermute | solution.py:258
  39.6 20.0 %all-to-all-start = ((bf16[16,4,2688]{2,1,0:T(4,128)(2,1)}), bf16[16,4,2688]{2,1,0:T(4,128)(2,1)S(1)}, u32[]{:S(2)}, u32[]{:S(2)}) async-start(bf16[16,4,2688]{2,1,0:T(4,128)(2,1)} %broadcast_in_dim.2), calls=%async_computation | async-start | bytes 688128 | tf_op jit(solution)/shard_map/all_to_all | solution.py:260
  59.8 1.1 %copy-start = (f32[26,640]{1,0:T(8,128)S(1)}, f32[26,640]{1,0:T(8,128)}, u32[]{:S(2)}) copy-start(f32[26,640]{1,0:T(8,128)} %constant.45.clone.slow_sin) | copy-start | bytes 199684
  59.8 1.1 %copy-start.1 = (f32[26,640]{1,0:T(8,128)S(1)}, f32[26,640]{1,0:T(8,128)}, u32[]{:S(2)}) copy-start(f32[26,640]{1,0:T(8,128)} %constant.44.clone.slow_cos) | copy-start | bytes 199684

commit v3 on v2

--- a/solution.py
+++ b/solution.py
@@ -23,8 +23,7 @@
 SENT = WIDTH + LANE
 QUICK = 4
 SLOW = (LAGS + QUICK - 1) // QUICK
-GROUP = 13
-STEPS = SLOW // GROUP
+CHUNKS = (4, 8, 8, 4, 2)
 
 epsilon = 1e-05
 
@@ -151,6 +150,25 @@
     )
 
 
+def repeat_kernel(one_ref, many_ref):
+    sent = one_ref[...]
+    for copy in range(many_ref.shape[0]):
+        many_ref[copy] = sent
+
+
+def repeat(one, copies):
+    vmem = pl.BlockSpec(memory_space=pltpu.VMEM)
+    return pl.pallas_call(
+        repeat_kernel,
+        out_shape=jax.ShapeDtypeStruct((copies,) + one.shape, one.dtype),
+        in_specs=[vmem],
+        out_specs=vmem,
+        compiler_params=pltpu.CompilerParams(vmem_limit_bytes=8 * 2**20),
+        cost_estimate=pl.CostEstimate(flops=2 * 10**10, bytes_accessed=10**6, transcendentals=0),
+        name="repeat",
+    )(one)
+
+
 def rotate(values, cosine, sine, window):
     real = values[:, 2 * NF * window : 2 * NF * window + NF]
     imag = values[:, 2 * NF * window + NF : 2 * NF * (window + 1)]
@@ -188,54 +206,67 @@
     )(place, near, far, *map(jnp.asarray, step_table()))
 
 
-def correlate_kernel(first_ref, partner_ref, weight_ref, slow_cos, slow_sin, out_ref, first_wide, turned, scale):
-    rows = first_ref.shape[0]
-
-    @pl.when(pl.program_id(0) == 0)
-    def _():
-        first = first_ref[...]
-        counts = lax.dot_general(
-            first[:, WIDTH:], weight_ref[...], (((1,), (1,)), ((), ())), preferred_element_type=jnp.float32
+def correlate_kernel(
+    first_ref, partner_ref, weight_ref, slow_cos, slow_sin, out_hbm,
+    first_wide, first_tail, turned, staged, sent,
+):
+    rows = first_wide.shape[0]
+    for s in range(rows // OWN):
+        own = first_ref[s].astype(jnp.float32)
+        first_wide[OWN * s : OWN * (s + 1), :] = own[:, :WIDTH]
+        first_tail[OWN * s : OWN * (s + 1), :] = own[:, WIDTH:]
+    counts = lax.dot_general(
+        first_tail[...].astype(jnp.bfloat16), weight_ref[...], (((1,), (1,)), ((), ())),
+        preferred_element_type=jnp.float32,
+    )
+    scale = (1.0 / math.sqrt(NF)) / jnp.maximum(counts, 1.0)
+
+    def turn(n):
+        for g in range(CHUNKS[n]):
+            stride = sum(CHUNKS[:n]) + g
+            cosine, sine = slow_cos[stride : stride + 1, :], slow_sin[stride : stride + 1, :]
+            at = slice(rows * g, rows * (g + 1))
+            for w in range(WIN):
+                for part, value in enumerate(rotate(first_wide, cosine, sine, w)):
+                    start = NF * (WIN * w + part)
+                    turned[n % 2, at, start : start + NF] = value.astype(jnp.bfloat16)
+
+    copies = []
+    turn(0)
+    for n, size in enumerate(CHUNKS):
+        result = jnp.dot(
+            turned[n % 2, : rows * size, :], partner_ref[...], preferred_element_type=jnp.float32
         )
-        scale[...] = (1.0 / math.sqrt(NF)) / jnp.maximum(counts, 1.0)
-        first_wide[...] = first[:, :WIDTH].astype(jnp.float32)
-
-    for g in range(GROUP):
-        stride = pl.program_id(0) * GROUP + g
-        cosine, sine = slow_cos[pl.ds(stride, 1), :], slow_sin[pl.ds(stride, 1), :]
-        at = slice(rows * g, rows * (g + 1))
-        for w in range(WIN):
-            for part, value in enumerate(rotate(first_wide, cosine, sine, w)):
-                start = NF * (WIN * w + part)
-                turned[at, start : start + NF] = value.astype(jnp.bfloat16)
-    result = jnp.dot(turned[...], partner_ref[...], preferred_element_type=jnp.float32)
-    factor = scale[...]
-    for g in range(GROUP):
-        for q in range(QUICK):
-            out_ref[QUICK * g + q] = (
-                result[rows * g : rows * (g + 1), LANE * q : LANE * (q + 1)] * factor
-            )
+        if n + 1 < len(CHUNKS):
+            turn(n + 1)
+        begin = sum(CHUNKS[:n]) * QUICK
+        end = min(begin + size * QUICK, LAGS)
+        for lag in range(begin, end):
+            g, q = divmod(lag - begin, QUICK)
+            staged[lag] = result[rows * g : rows * (g + 1), LANE * q : LANE * (q + 1)] * scale
+        copy = pltpu.make_async_copy(
+            staged.at[pl.ds(begin, end - begin)], out_hbm.at[pl.ds(begin, end - begin)], sent.at[n]
+        )
+        copy.start()
+        copies.append(copy)
+    for copy in copies:
+        copy.wait()
 
 
 def correlate(first, partner, weight):
-    rows = first.shape[0]
-    whole = lambda shape: pl.BlockSpec(shape, lambda i: (0,) * len(shape))
+    rows = first.shape[0] * first.shape[1]
+    vmem = pl.BlockSpec(memory_space=pltpu.VMEM)
     return pl.pallas_call(
         correlate_kernel,
-        grid=(STEPS,),
         out_shape=jax.ShapeDtypeStruct((LAGS, rows, LANE), jnp.float32),
-        in_specs=[
-            whole((rows, SENT)),
-            whole(partner.shape),
-            whole(weight.shape),
-            whole((SLOW, NF)),
-            whole((SLOW, NF)),
-        ],
-        out_specs=pl.BlockSpec((GROUP * QUICK, rows, LANE), lambda i: (i, 0, 0)),
+        in_specs=[vmem] * 5,
+        out_specs=pl.BlockSpec(memory_space=pltpu.HBM),
         scratch_shapes=[
             pltpu.VMEM((rows, WIDTH), jnp.float32),
-            pltpu.VMEM((GROUP * rows, WIDTH), jnp.bfloat16),
             pltpu.VMEM((rows, LANE), jnp.float32),
+            pltpu.VMEM((2, max(CHUNKS) * rows, WIDTH), jnp.bfloat16),
+            pltpu.VMEM((LAGS, rows, LANE), jnp.float32),
+            pltpu.SemaphoreType.DMA((len(CHUNKS),)),
         ],
         compiler_params=pltpu.CompilerParams(vmem_limit_bytes=36 * 2**20),
         name="correlate",
@@ -256,8 +287,8 @@
     lines = [list(range(ring)), list(range(ring, row_count))]
     near = lax.all_to_all(many, "row", 0, 0, axis_index_groups=lines).reshape(ring * OWN, SENT)
     far = lax.ppermute(near, "row", [(r, (r + ring) % row_count) for r in range(row_count)])
-    shared = jnp.broadcast_to(mine[None], (col_count, OWN, SENT))
-    first = lax.all_to_all(shared, "col", 0, 0).reshape(col_count * OWN, SENT)
+    shared = repeat(mine, col_count)
+    first = lax.all_to_all(shared, "col", 0, 0)
     partner, weight = turn_partner(place, near, far)
     return correlate(first, partner, weight)
 

time: 68 us -> 66.4 us (0.976)
  waiting for transfers between devices: 18.2 us -> 15.4 us
  local copies, waits for them, and re-layouts: 1.01 us -> 1.81 us
    all_to_all x1, waiting for transfers between devices: 7.86 us -> 5.04 us  [local(): first = lax.all_to_all(shared, 'col', 0, 0)]
    unnamed x8 -> x12, local copies, waits for them, and re-layouts: 0.02 us -> 1.73 us
    broadcast_in_dim x1 -> x0, local copies, waits for them, and re-layouts: 0.82 us -> none  [local(): shared = jnp.broadcast_to(mine[None], (col_count, OWN, SENT))]
    pallas_call x1 -> x2, Pallas kernels: 6.12 us -> 6.6 us  [the longest x1 5.85 us: correlate(): pl.pallas_call(correlate_kernel, out_shape=jax.ShapeDtypeStruct((LAGS, ro...]
  transfers between devices with their start and end apart: 4 -> 4, of which waited for: 2 -> 2; matrix products, arithmetic and copies ran while one was open for 1% -> 0% of each run, Pallas kernels for 0% -> 3%
where the time goes in v3:
time: 66.4 us; the launch traced here: 65.4 us
  starting transfers between devices  37.8 us (57%)
  waiting for transfers between devices  15.4 us (23%)
  Pallas kernels  10.3 us (16%)
  local copies, waits for them, and re-layouts  1.81 us (3%)
    all_to_all x1, starting transfers between devices, local(): lax.all_to_all(many, 'row', 0, 0, axis_index_groups=lines)  15.8 us
    all_to_all x1, starting transfers between devices, local(): first = lax.all_to_all(shared, 'col', 0, 0)  12.2 us
    all_to_all x1, waiting for transfers between devices, local(): lax.all_to_all(many, 'row', 0, 0, axis_index_groups=lines)  10.3 us
    pallas_call x1, Pallas kernels, correlate(): pl.pallas_call(correlate_kernel, out_shape=jax.ShapeDtypeStruct((LAGS, ro...  5.85 us
    ppermute x1, starting transfers between devices, local(): mine = lax.ppermute(own, ('row', 'col'), moves)  5.28 us
    all_to_all x1, waiting for transfers between devices, local(): first = lax.all_to_all(shared, 'col', 0, 0)  5.04 us
    ppermute x1, starting transfers between devices, local(): lax.ppermute(near, 'row', [(r, (r + ring) % row_count) for r in range(row...  4.65 us
    pallas_call x1, Pallas kernels, whiten(): pl.pallas_call(whiten_kernel, out_shape=(jax.ShapeDtypeStruct((copies, OW...  2.65 us
  transfers between devices with their start and end apart: 4, of which 2 were waited for; matrix products, arithmetic and copies ran while one was open for 0% of the time, Pallas kernels for 3%

profile of v3, /device:TPU:1, one launch (start us, length us, event | category | flops | bytes accessed | tf_op | source)
XLA Modules:
  0.0 65.4 jit_solution(13318604866679467545)
XLA Ops:
  0.0 2.6 %whiten.1 = (bf16[16,4,2688]{2,1,0:T(4,128)(2,1)}, bf16[4,2688]{1,0:T(4,128)(2,1)}) custom-call(s32[1,4]{1,0:T(1,128)} %alive_hbm.1, s32[1,2,4]{2,1,0:T(2,128)} %bitcast.2, f32[1,4,2,1536]{3,2,1,0:T(2,128)} %traces_hbm.1, bf16[128,1280]{1,0:T(8,128)(2,1)} %constant.38.clone.high_hbm, bf16[128,1280]{1,0:T(8,128)(2,1)} %constant.39.clone.low_hbm, ...), custom_call_target="tpu_custom_call" | custom-call | tf_op jit(solution)/shard_map/whiten/pallas_call | solution.py:129
  2.7 15.8 %all-to-all-start.1 = ((bf16[16,4,2688]{2,1,0:T(4,128)(2,1)}), bf16[16,4,2688]{2,1,0:T(4,128)(2,1)S(1)}, u32[]{:S(2)}, u32[]{:S(2)}) async-start(bf16[16,4,2688]{2,1,0:T(4,128)(2,1)} %get-tuple-element.10), calls=%async_computation.1 | async-start | bytes 688128 | tf_op jit(solution)/shard_map/all_to_all | solution.py:288
  18.4 5.3 %collective-permute-start = (bf16[4,2688]{1,0:T(4,128)(2,1)}, bf16[4,2688]{1,0:T(4,128)(2,1)S(1)}, u32[]{:S(2)}, u32[]{:S(2)}) collective-permute-start(bf16[4,2688]{1,0:T(4,128)(2,1)} %get-tuple-element.9), channel_id=1, source_target_pairs={{0,0},{1,32},{2,64},{3,96},{4,128},{5,160},{6,192},{7,224},{8,256}... | collective-permute-start | bytes 64520 | tf_op jit(solution)/shard_map/ppermute | solution.py:286
  23.7 10.3 %all-to-all-done.1 = bf16[16,4,2688]{2,1,0:T(4,128)(2,1)S(1)} async-done(((bf16[16,4,2688]{2,1,0:T(4,128)(2,1)}), bf16[16,4,2688]{2,1,0:T(4,128)(2,1)S(1)}, u32[]{:S(2)}, u32[]{:S(2)}) %all-to-all-start.1) | async-done | bytes 344096 | tf_op jit(solution)/shard_map/all_to_all | solution.py:288
  34.0 0.1 reshape.7.near_ref
  34.1 0.0 copy-start.4
  34.1 0.0 copy-start.5
  34.1 4.7 %collective-permute-start.1 = (bf16[64,2688]{1,0:T(8,128)(2,1)S(1)}, bf16[64,2688]{1,0:T(8,128)(2,1)S(1)}, u32[]{:S(2)}, u32[]{:S(2)}) collective-permute-start(bf16[64,2688]{1,0:T(8,128)(2,1)S(1)} %reshape.7.near_ref), channel_id=1, source_target_pairs={{0,256},{16,272},{32,288},{48,304},{64,320},{80,336},{96,352},{112... | collective-permute-start | bytes 1032200 | tf_op jit(solution)/shard_map/ppermute | solution.py:289
  38.8 0.0 collective-permute-done.one_ref
  38.8 0.8 %repeat.1 = bf16[16,4,2688]{2,1,0:T(4,128)(2,1)} custom-call(bf16[4,2688]{1,0:T(4,128)(2,1)S(1)} %collective-permute-done.one_ref), custom_call_target="tpu_custom_call" | custom-call | flops 20000000000 | bytes 1000000 | tf_op jit(solution)/shard_map/repeat/pallas_call | solution.py:161
  39.6 12.2 %all-to-all-start = ((bf16[16,4,2688]{2,1,0:T(4,128)(2,1)}), bf16[16,4,2688]{2,1,0:T(4,128)(2,1)S(1)}, u32[]{:S(2)}, u32[]{:S(2)}) async-start(bf16[16,4,2688]{2,1,0:T(4,128)(2,1)} %repeat.1), calls=%async_computation | async-start | bytes 688128 | tf_op jit(solution)/shard_map/all_to_all | solution.py:291
  51.7 0.0 collective-permute-done.1.far_ref
  51.7 0.0 copy-start.2
  51.7 0.7 %copy-done.2 = bf16[64,2688]{1,0:T(8,128)(2,1)} copy-done((bf16[64,2688]{1,0:T(8,128)(2,1)}, bf16[64,2688]{1,0:T(8,128)(2,1)S(1)}, u32[]{:S(2)}) %copy-start.2) | copy-done | bytes 344088
  52.5 0.0 copy-done.4
  52.5 0.0 copy-done.5
  52.5 0.0 copy-start.3
  52.5 1.0 %copy-done.3 = bf16[64,2688]{1,0:T(8,128)(2,1)S(1)} copy-done((bf16[64,2688]{1,0:T(8,128)(2,1)S(1)}, bf16[64,2688]{1,0:T(8,128)(2,1)}, u32[]{:S(2)}) %copy-start.3) | copy-done | bytes 344088
  53.5 0.0 copy-start
  53.5 0.0 copy-start.1
  53.5 1.1 %turn_partner.1 = (bf16[2560,512]{1,0:T(8,128)(2,1)S(1)}, bf16[128,128]{1,0:T(8,128)(2,1)S(1)}) custom-call(s32[1]{0:T(128)} %bitcast.1.place_ref, bf16[64,2688]{1,0:T(8,128)(2,1)S(1)} %reshape.7.near_ref, bf16[64,2688]{1,0:T(8,128)(2,1)S(1)} %copy-done.3, f32[4,640]{1,0:T(4,128)S(1)} %copy-done.5, f32[4,640]{1,0:T(4,128)S(1)} %copy-done.4), custom_call_target="tpu_custom_call" | custom-call | flops 20000000000 | bytes 5000000 | tf_op jit(solution)/shard_map/turn_partner/pallas_call | solution.py:195
  54.6 5.0 %all-to-all-done.first_ref = bf16[16,4,2688]{2,1,0:T(4,128)(2,1)S(1)} async-done(((bf16[16,4,2688]{2,1,0:T(4,128)(2,1)}), bf16[16,4,2688]{2,1,0:T(4,128)(2,1)S(1)}, u32[]{:S(2)}, u32[]{:S(2)}) %all-to-all-start) | async-done | bytes 344096 | tf_op jit(solution)/shard_map/all_to_all | solution.py:291
  59.6 0.0 copy-done
  59.6 0.0 copy-done.1
  59.6 5.8 %correlate.1 = f32[101,64,128]{2,1,0:T(8,128)} custom-call(bf16[16,4,2688]{2,1,0:T(4,128)(2,1)S(1)} %all-to-all-done.first_ref, bf16[2560,512]{1,0:T(8,128)(2,1)S(1)} %get-tuple-element.11.partner_ref, bf16[128,128]{1,0:T(8,128)(2,1)S(1)} %get-tuple-element.12.weight_ref, f32[26,640]{1,0:T(8,128)S(1)} %copy-done.1, f32[26,640]{1,0:T(8,128)S(1)} %copy-done), custom_call_target="tpu_custom_call" | custom-call | tf_op jit(solution)/shard_map/correlate/pallas_call | solution.py:259
Async XLA Ops:
  2.7 31.4 %all-to-all-start.1 = ((bf16[16,4,2688]{2,1,0:T(4,128)(2,1)}), bf16[16,4,2688]{2,1,0:T(4,128)(2,1)S(1)}, u32[]{:S(2)}, u32[]{:S(2)}) async-start(bf16[16,4,2688]{2,1,0:T(4,128)(2,1)} %get-tuple-element.10), calls=%async_computation.1 | async-start | bytes 688128 | tf_op jit(solution)/shard_map/all_to_all | solution.py:288
  18.4 20.4 %collective-permute-start = (bf16[4,2688]{1,0:T(4,128)(2,1)}, bf16[4,2688]{1,0:T(4,128)(2,1)S(1)}, u32[]{:S(2)}, u32[]{:S(2)}) collective-permute-start(bf16[4,2688]{1,0:T(4,128)(2,1)} %get-tuple-element.9), channel_id=1, source_target_pairs={{0,0},{1,32},{2,64},{3,96},{4,128},{5,160},{6,192},{7,224},{8,256}... | collective-permute-start | bytes 64520 | tf_op jit(solution)/shard_map/ppermute | solution.py:286
  34.1 18.4 %copy-start.4 = (f32[4,640]{1,0:T(4,128)S(1)}, f32[4,640]{1,0:T(4,128)}, u32[]{:S(2)}) copy-start(f32[4,640]{1,0:T(4,128)} %constant.43.clone.quick_sin) | copy-start | bytes 30724
  34.1 18.3 %copy-start.5 = (f32[4,640]{1,0:T(4,128)S(1)}, f32[4,640]{1,0:T(4,128)}, u32[]{:S(2)}) copy-start(f32[4,640]{1,0:T(4,128)} %constant.42.clone.quick_cos) | copy-start | bytes 30724
  34.1 17.6 %collective-permute-start.1 = (bf16[64,2688]{1,0:T(8,128)(2,1)S(1)}, bf16[64,2688]{1,0:T(8,128)(2,1)S(1)}, u32[]{:S(2)}, u32[]{:S(2)}) collective-permute-start(bf16[64,2688]{1,0:T(8,128)(2,1)S(1)} %reshape.7.near_ref), channel_id=1, source_target_pairs={{0,256},{16,272},{32,288},{48,304},{64,320},{80,336},{96,352},{112... | collective-permute-start | bytes 1032200 | tf_op jit(solution)/shard_map/ppermute | solution.py:289
  39.6 20.0 %all-to-all-start = ((bf16[16,4,2688]{2,1,0:T(4,128)(2,1)}), bf16[16,4,2688]{2,1,0:T(4,128)(2,1)S(1)}, u32[]{:S(2)}, u32[]{:S(2)}) async-start(bf16[16,4,2688]{2,1,0:T(4,128)(2,1)} %repeat.1), calls=%async_computation | async-start | bytes 688128 | tf_op jit(solution)/shard_map/all_to_all | solution.py:291
  51.7 0.7 %copy-start.2 = (bf16[64,2688]{1,0:T(8,128)(2,1)}, bf16[64,2688]{1,0:T(8,128)(2,1)S(1)}, u32[]{:S(2)}) copy-start(bf16[64,2688]{1,0:T(8,128)(2,1)S(1)} %collective-permute-done.1.far_ref) | copy-start | bytes 1032196
  52.5 1.0 %copy-start.3 = (bf16[64,2688]{1,0:T(8,128)(2,1)S(1)}, bf16[64,2688]{1,0:T(8,128)(2,1)}, u32[]{:S(2)}) copy-start(bf16[64,2688]{1,0:T(8,128)(2,1)} %copy-done.2) | copy-start | bytes 1032196
  53.5 6.1 %copy-start = (f32[26,640]{1,0:T(8,128)S(1)}, f32[26,640]{1,0:T(8,128)}, u32[]{:S(2)}) copy-start(f32[26,640]{1,0:T(8,128)} %constant.45.clone.slow_sin) | copy-start | bytes 199684
  53.5 6.1 %copy-start.1 = (f32[26,640]{1,0:T(8,128)S(1)}, f32[26,640]{1,0:T(8,128)}, u32[]{:S(2)}) copy-start(f32[26,640]{1,0:T(8,128)} %constant.44.clone.slow_cos) | copy-start | bytes 199684

commit v4 on v3

--- a/solution.py
+++ b/solution.py
@@ -177,7 +177,10 @@
 
 def partner_kernel(place_ref, near_ref, far_ref, quick_cos, quick_sin, turned_ref, weight_ref):
     lower = place_ref[0] == 0
-    near, far = near_ref[...], far_ref[...]
+    middle = near_ref.shape[0] // 2
+    near, far = (
+        jnp.concatenate([ref[middle:, :], ref[:middle, :]], axis=0) for ref in (near_ref, far_ref)
+    )
     block = jnp.concatenate([jnp.where(lower, near, far), jnp.where(lower, far, near)], axis=0)
     weight_ref[...] = block[:, WIDTH:]
     wide = block[:, :WIDTH].astype(jnp.float32)
@@ -284,7 +287,8 @@
         for c in range(col_count)
     ]
     mine = lax.ppermute(own, ("row", "col"), moves)
-    lines = [list(range(ring)), list(range(ring, row_count))]
+    turned = [(z + ring // 2) % ring for z in range(ring)]
+    lines = [turned, [ring + z for z in turned]]
     near = lax.all_to_all(many, "row", 0, 0, axis_index_groups=lines).reshape(ring * OWN, SENT)
     far = lax.ppermute(near, "row", [(r, (r + ring) % row_count) for r in range(row_count)])
     shared = repeat(mine, col_count)

time: 66.4 us -> 65.5 us (0.986)
  starting transfers between devices: 37.8 us -> 34 us
  waiting for transfers between devices: 15.4 us -> 18.8 us
    all_to_all x1, starting transfers between devices: 12.2 us -> 7.71 us  [local(): first = lax.all_to_all(shared, 'col', 0, 0)]
    all_to_all x1, waiting for transfers between devices: 10.3 us -> 13.7 us  [local(): lax.all_to_all(many, 'row', 0, 0, axis_index_groups=lines)]
    all_to_all x1, starting transfers between devices: 15.8 us -> 19.1 us  [local(): lax.all_to_all(many, 'row', 0, 0, axis_index_groups=lines)]
    ppermute x1, starting transfers between devices: 5.28 us -> 3.3 us  [local(): mine = lax.ppermute(own, ('row', 'col'), moves)]
    ppermute x1, starting transfers between devices: 4.65 us -> 3.9 us  [local(): lax.ppermute(near, 'row', [(r, (r + ring) % row_count) for r in range(row...]
where the time goes in v4:
time: 65.5 us; the launch traced here: 65.1 us
  starting transfers between devices  34 us (52%)
  waiting for transfers between devices  18.8 us (29%)
  Pallas kernels  10.3 us (16%)
  local copies, waits for them, and re-layouts  1.81 us (3%)
    all_to_all x1, starting transfers between devices, local(): lax.all_to_all(many, 'row', 0, 0, axis_index_groups=lines)  19.1 us
    all_to_all x1, waiting for transfers between devices, local(): lax.all_to_all(many, 'row', 0, 0, axis_index_groups=lines)  13.7 us
    all_to_all x1, starting transfers between devices, local(): first = lax.all_to_all(shared, 'col', 0, 0)  7.71 us
    pallas_call x1, Pallas kernels, correlate(): pl.pallas_call(correlate_kernel, out_shape=jax.ShapeDtypeStruct((LAGS, ro...  5.85 us
    all_to_all x1, waiting for transfers between devices, local(): first = lax.all_to_all(shared, 'col', 0, 0)  5.06 us
    ppermute x1, starting transfers between devices, local(): lax.ppermute(near, 'row', [(r, (r + ring) % row_count) for r in range(row...  3.9 us
    ppermute x1, starting transfers between devices, local(): mine = lax.ppermute(own, ('row', 'col'), moves)  3.3 us
    pallas_call x1, Pallas kernels, whiten(): pl.pallas_call(whiten_kernel, out_shape=(jax.ShapeDtypeStruct((copies, OW...  2.65 us
  transfers between devices with their start and end apart: 4, of which 2 were waited for; matrix products, arithmetic and copies ran while one was open for 0% of the time, Pallas kernels for 3%

profile of v4, /device:TPU:1, one launch (start us, length us, event | category | flops | bytes accessed | tf_op | source)
XLA Modules:
  0.0 65.1 jit_solution(10069071711955225422)
XLA Ops:
  0.0 2.6 %whiten.1 = (bf16[16,4,2688]{2,1,0:T(4,128)(2,1)}, bf16[4,2688]{1,0:T(4,128)(2,1)}) custom-call(s32[1,4]{1,0:T(1,128)} %alive_hbm.1, s32[1,2,4]{2,1,0:T(2,128)} %bitcast.2, f32[1,4,2,1536]{3,2,1,0:T(2,128)} %traces_hbm.1, bf16[128,1280]{1,0:T(8,128)(2,1)} %constant.38.clone.high_hbm, bf16[128,1280]{1,0:T(8,128)(2,1)} %constant.39.clone.low_hbm, ...), custom_call_target="tpu_custom_call" | custom-call | tf_op jit(solution)/shard_map/whiten/pallas_call | solution.py:129
  2.7 19.1 %all-to-all-start.1 = ((bf16[16,4,2688]{2,1,0:T(4,128)(2,1)}), bf16[16,4,2688]{2,1,0:T(4,128)(2,1)S(1)}, u32[]{:S(2)}, u32[]{:S(2)}) async-start(bf16[16,4,2688]{2,1,0:T(4,128)(2,1)} %get-tuple-element.10), calls=%async_computation.1 | async-start | bytes 688128 | tf_op jit(solution)/shard_map/all_to_all | solution.py:292
  21.8 3.3 %collective-permute-start = (bf16[4,2688]{1,0:T(4,128)(2,1)}, bf16[4,2688]{1,0:T(4,128)(2,1)S(1)}, u32[]{:S(2)}, u32[]{:S(2)}) collective-permute-start(bf16[4,2688]{1,0:T(4,128)(2,1)} %get-tuple-element.9), channel_id=1, source_target_pairs={{0,0},{1,32},{2,64},{3,96},{4,128},{5,160},{6,192},{7,224},{8,256}... | collective-permute-start | bytes 64520 | tf_op jit(solution)/shard_map/ppermute | solution.py:289
  25.1 13.7 %all-to-all-done.1 = bf16[16,4,2688]{2,1,0:T(4,128)(2,1)S(1)} async-done(((bf16[16,4,2688]{2,1,0:T(4,128)(2,1)}), bf16[16,4,2688]{2,1,0:T(4,128)(2,1)S(1)}, u32[]{:S(2)}, u32[]{:S(2)}) %all-to-all-start.1) | async-done | bytes 344096 | tf_op jit(solution)/shard_map/all_to_all | solution.py:292
  38.8 0.1 reshape.7.near_ref
  38.9 0.0 copy-start.4
  38.9 0.0 copy-start.5
  39.0 3.9 %collective-permute-start.1 = (bf16[64,2688]{1,0:T(8,128)(2,1)S(1)}, bf16[64,2688]{1,0:T(8,128)(2,1)S(1)}, u32[]{:S(2)}, u32[]{:S(2)}) collective-permute-start(bf16[64,2688]{1,0:T(8,128)(2,1)S(1)} %reshape.7.near_ref), channel_id=1, source_target_pairs={{0,256},{16,272},{32,288},{48,304},{64,320},{80,336},{96,352},{112... | collective-permute-start | bytes 1032200 | tf_op jit(solution)/shard_map/ppermute | solution.py:293
  42.9 0.0 collective-permute-done.one_ref
  42.9 0.8 %repeat.1 = bf16[16,4,2688]{2,1,0:T(4,128)(2,1)} custom-call(bf16[4,2688]{1,0:T(4,128)(2,1)S(1)} %collective-permute-done.one_ref), custom_call_target="tpu_custom_call" | custom-call | flops 20000000000 | bytes 1000000 | tf_op jit(solution)/shard_map/repeat/pallas_call | solution.py:161
  43.6 7.7 %all-to-all-start = ((bf16[16,4,2688]{2,1,0:T(4,128)(2,1)}), bf16[16,4,2688]{2,1,0:T(4,128)(2,1)S(1)}, u32[]{:S(2)}, u32[]{:S(2)}) async-start(bf16[16,4,2688]{2,1,0:T(4,128)(2,1)} %repeat.1), calls=%async_computation | async-start | bytes 688128 | tf_op jit(solution)/shard_map/all_to_all | solution.py:295
  51.3 0.0 collective-permute-done.1.far_ref
  51.4 0.0 copy-start.2
  51.4 0.7 %copy-done.2 = bf16[64,2688]{1,0:T(8,128)(2,1)} copy-done((bf16[64,2688]{1,0:T(8,128)(2,1)}, bf16[64,2688]{1,0:T(8,128)(2,1)S(1)}, u32[]{:S(2)}) %copy-start.2) | copy-done | bytes 344088
  52.1 0.0 copy-done.4
  52.1 0.0 copy-done.5
  52.1 0.0 copy-start.3
  52.1 1.0 %copy-done.3 = bf16[64,2688]{1,0:T(8,128)(2,1)S(1)} copy-done((bf16[64,2688]{1,0:T(8,128)(2,1)S(1)}, bf16[64,2688]{1,0:T(8,128)(2,1)}, u32[]{:S(2)}) %copy-start.3) | copy-done | bytes 344088
  53.1 0.0 copy-start
  53.1 0.0 copy-start.1
  53.1 1.1 %turn_partner.1 = (bf16[2560,512]{1,0:T(8,128)(2,1)S(1)}, bf16[128,128]{1,0:T(8,128)(2,1)S(1)}) custom-call(s32[1]{0:T(128)} %bitcast.1.place_ref, bf16[64,2688]{1,0:T(8,128)(2,1)S(1)} %reshape.7.near_ref, bf16[64,2688]{1,0:T(8,128)(2,1)S(1)} %copy-done.3, f32[4,640]{1,0:T(4,128)S(1)} %copy-done.5, f32[4,640]{1,0:T(4,128)S(1)} %copy-done.4), custom_call_target="tpu_custom_call" | custom-call | flops 20000000000 | bytes 5000000 | tf_op jit(solution)/shard_map/turn_partner/pallas_call | solution.py:198
  54.2 5.1 %all-to-all-done.first_ref = bf16[16,4,2688]{2,1,0:T(4,128)(2,1)S(1)} async-done(((bf16[16,4,2688]{2,1,0:T(4,128)(2,1)}), bf16[16,4,2688]{2,1,0:T(4,128)(2,1)S(1)}, u32[]{:S(2)}, u32[]{:S(2)}) %all-to-all-start) | async-done | bytes 344096 | tf_op jit(solution)/shard_map/all_to_all | solution.py:295
  59.2 0.0 copy-done
  59.2 0.0 copy-done.1
  59.2 5.8 %correlate.1 = f32[101,64,128]{2,1,0:T(8,128)} custom-call(bf16[16,4,2688]{2,1,0:T(4,128)(2,1)S(1)} %all-to-all-done.first_ref, bf16[2560,512]{1,0:T(8,128)(2,1)S(1)} %get-tuple-element.11.partner_ref, bf16[128,128]{1,0:T(8,128)(2,1)S(1)} %get-tuple-element.12.weight_ref, f32[26,640]{1,0:T(8,128)S(1)} %copy-done.1, f32[26,640]{1,0:T(8,128)S(1)} %copy-done), custom_call_target="tpu_custom_call" | custom-call | tf_op jit(solution)/shard_map/correlate/pallas_call | solution.py:262
Async XLA Ops:
  2.7 36.2 %all-to-all-start.1 = ((bf16[16,4,2688]{2,1,0:T(4,128)(2,1)}), bf16[16,4,2688]{2,1,0:T(4,128)(2,1)S(1)}, u32[]{:S(2)}, u32[]{:S(2)}) async-start(bf16[16,4,2688]{2,1,0:T(4,128)(2,1)} %get-tuple-element.10), calls=%async_computation.1 | async-start | bytes 688128 | tf_op jit(solution)/shard_map/all_to_all | solution.py:292
  21.8 21.1 %collective-permute-start = (bf16[4,2688]{1,0:T(4,128)(2,1)}, bf16[4,2688]{1,0:T(4,128)(2,1)S(1)}, u32[]{:S(2)}, u32[]{:S(2)}) collective-permute-start(bf16[4,2688]{1,0:T(4,128)(2,1)} %get-tuple-element.9), channel_id=1, source_target_pairs={{0,0},{1,32},{2,64},{3,96},{4,128},{5,160},{6,192},{7,224},{8,256}... | collective-permute-start | bytes 64520 | tf_op jit(solution)/shard_map/ppermute | solution.py:289
  38.9 13.2 %copy-start.4 = (f32[4,640]{1,0:T(4,128)S(1)}, f32[4,640]{1,0:T(4,128)}, u32[]{:S(2)}) copy-start(f32[4,640]{1,0:T(4,128)} %constant.43.clone.quick_sin) | copy-start | bytes 30724
  38.9 13.1 %copy-start.5 = (f32[4,640]{1,0:T(4,128)S(1)}, f32[4,640]{1,0:T(4,128)}, u32[]{:S(2)}) copy-start(f32[4,640]{1,0:T(4,128)} %constant.42.clone.quick_cos) | copy-start | bytes 30724
  39.0 12.4 %collective-permute-start.1 = (bf16[64,2688]{1,0:T(8,128)(2,1)S(1)}, bf16[64,2688]{1,0:T(8,128)(2,1)S(1)}, u32[]{:S(2)}, u32[]{:S(2)}) collective-permute-start(bf16[64,2688]{1,0:T(8,128)(2,1)S(1)} %reshape.7.near_ref), channel_id=1, source_target_pairs={{0,256},{16,272},{32,288},{48,304},{64,320},{80,336},{96,352},{112... | collective-permute-start | bytes 1032200 | tf_op jit(solution)/shard_map/ppermute | solution.py:293
  43.6 15.6 %all-to-all-start = ((bf16[16,4,2688]{2,1,0:T(4,128)(2,1)}), bf16[16,4,2688]{2,1,0:T(4,128)(2,1)S(1)}, u32[]{:S(2)}, u32[]{:S(2)}) async-start(bf16[16,4,2688]{2,1,0:T(4,128)(2,1)} %repeat.1), calls=%async_computation | async-start | bytes 688128 | tf_op jit(solution)/shard_map/all_to_all | solution.py:295
  51.4 0.7 %copy-start.2 = (bf16[64,2688]{1,0:T(8,128)(2,1)}, bf16[64,2688]{1,0:T(8,128)(2,1)S(1)}, u32[]{:S(2)}) copy-start(bf16[64,2688]{1,0:T(8,128)(2,1)S(1)} %collective-permute-done.1.far_ref) | copy-start | bytes 1032196
  52.1 1.0 %copy-start.3 = (bf16[64,2688]{1,0:T(8,128)(2,1)S(1)}, bf16[64,2688]{1,0:T(8,128)(2,1)}, u32[]{:S(2)}) copy-start(bf16[64,2688]{1,0:T(8,128)(2,1)} %copy-done.2) | copy-start | bytes 1032196
  53.1 6.1 %copy-start = (f32[26,640]{1,0:T(8,128)S(1)}, f32[26,640]{1,0:T(8,128)}, u32[]{:S(2)}) copy-start(f32[26,640]{1,0:T(8,128)} %constant.45.clone.slow_sin) | copy-start | bytes 199684
  53.1 6.1 %copy-start.1 = (f32[26,640]{1,0:T(8,128)S(1)}, f32[26,640]{1,0:T(8,128)}, u32[]{:S(2)}) copy-start(f32[26,640]{1,0:T(8,128)} %constant.44.clone.slow_cos) | copy-start | bytes 199684
